TPU v7x, 256 devices: a whole 4x4x8 slice. The times are simulated.
256 devices in a mesh: roll: 32 (over y, z_hi, x), head: 8 (over z_lo, core).
Axes of the slice: x: 4, y: 4, z: 8 (z_hi: 2, z_lo: 4; z = z_hi * 4 + z_lo), core: 2. Of those that a mesh axis runs over, the one named last changes fastest.
Arguments:
- queries: bfloat16 [8192, 8192], P(('roll', 'head')), may hold values from -130 to 130
- keys: bfloat16 [8192, 1024], P(('roll', 'head')), may hold values from -7 to 7
- values: bfloat16 [8192, 1024], P(('roll', 'head')), may hold values from -6 to 6
- cotangent: bfloat16 [8192, 8192], P(('roll', 'head')), may hold values from -6 to 6
- doc_keys: bfloat16 [8192, 1024], P('roll', 'head'), may hold values from -6 to 6
- doc_values: bfloat16 [8192, 1024], P('roll', 'head'), may hold values from -6 to 6
- citations: int32 [32, 16], replicated, may hold values from 0 to 63, as said below
- block_lists: int32 [64, 4], P('roll'), may hold values from 0 to 15, as said below
Outputs:
- attended: bfloat16 [8192, 8192], P(('roll', 'head'))
- query_grad: bfloat16 [8192, 8192], P(('roll', 'head'))
- key_grad: bfloat16 [8192, 1024], P(('roll', 'head'))
- value_grad: bfloat16 [8192, 1024], P(('roll', 'head'))
- doc_key_grad: float32 [8192, 1024], P('roll', 'head')
- doc_value_grad: float32 [8192, 1024], P('roll', 'head')
Inputs may be any that keep to these rules, and one draw needn't show every extreme that they name: `citations`: each row names 16 documents of 16 different owners; document d belongs to roll index d // 2. `block_lists`: each row names 4 different positions.
All inputs are finite; a program needn't handle non-finite values.
Results may differ from a plain program's by a relative error of at most 0.015.
Values may be sent and summed in bfloat16 or wider, within the bound.
A program may use at most 64 MiB of HBM per device.

v0:
```python
import math

import jax
import jax.numpy as jnp
from jax import lax
from jax.sharding import PartitionSpec as P

HD = 128
QH = 64
KVH = 8
BLOCK = 128
CITE = 16


def block_pass(query, grad_out, key_loc, value_loc, key_doc, value_doc, start):
    f = jnp.float32
    scale = 1.0 / math.sqrt(query.shape[-1])
    score_loc = jnp.einsum("igqd,jgd->gqij", query, key_loc, preferred_element_type=f) * scale
    rows_pos = start + jnp.arange(query.shape[0], dtype=jnp.int32)
    cols_pos = jnp.arange(key_loc.shape[0], dtype=jnp.int32)
    visible = cols_pos[None, :] <= rows_pos[:, None]
    score_loc = jnp.where(visible, score_loc, -jnp.inf)
    score_doc = jnp.einsum("igqd,jgd->gqij", query, key_doc, preferred_element_type=f) * scale
    top = jnp.maximum(jnp.max(score_loc, axis=-1), jnp.max(score_doc, axis=-1))[..., None]
    exp_loc = jnp.exp(score_loc - top)
    exp_doc = jnp.exp(score_doc - top)
    total = jnp.sum(exp_loc, axis=-1, keepdims=True) + jnp.sum(exp_doc, axis=-1, keepdims=True)
    prob_loc = exp_loc / total
    prob_doc = exp_doc / total
    weight_loc = prob_loc.astype(jnp.bfloat16)
    weight_doc = prob_doc.astype(jnp.bfloat16)
    output = jnp.einsum(
        "gqij,jgd->igqd", weight_loc, value_loc, preferred_element_type=f
    ) + jnp.einsum("gqij,jgd->igqd", weight_doc, value_doc, preferred_element_type=f)
    dprob_loc = jnp.einsum("igqd,jgd->gqij", grad_out, value_loc, preferred_element_type=f)
    dprob_doc = jnp.einsum("igqd,jgd->gqij", grad_out, value_doc, preferred_element_type=f)
    delta = jnp.sum(prob_loc * dprob_loc, axis=-1, keepdims=True) + jnp.sum(
        prob_doc * dprob_doc, axis=-1, keepdims=True
    )
    dscore_loc = (prob_loc * (dprob_loc - delta)).astype(jnp.bfloat16)
    dscore_doc = (prob_doc * (dprob_doc - delta)).astype(jnp.bfloat16)
    dquery = (
        jnp.einsum("gqij,jgd->igqd", dscore_loc, key_loc, preferred_element_type=f)
        + jnp.einsum("gqij,jgd->igqd", dscore_doc, key_doc, preferred_element_type=f)
    ) * scale
    dkey_loc = jnp.einsum("gqij,igqd->jgd", dscore_loc, query, preferred_element_type=f) * scale
    dvalue_loc = jnp.einsum("gqij,igqd->jgd", weight_loc, grad_out, preferred_element_type=f)
    dkey_doc = jnp.einsum("gqij,igqd->jgd", dscore_doc, query, preferred_element_type=f) * scale
    dvalue_doc = jnp.einsum("gqij,igqd->jgd", weight_doc, grad_out, preferred_element_type=f)
    return (
        output.astype(jnp.bfloat16),
        dquery.astype(jnp.bfloat16),
        dkey_loc,
        dvalue_loc,
        dkey_doc,
        dvalue_doc,
    )


def local(queries, keys, values, cotangent, doc_keys, doc_values, citations, block_lists):
    roll_index = lax.axis_index("roll")
    query_win, grad_win, key_win, value_win = (
        lax.all_to_all(queries, "head", split_axis=1, concat_axis=0, tiled=True),
        lax.all_to_all(cotangent, "head", split_axis=1, concat_axis=0, tiled=True),
        lax.all_to_all(keys, "head", split_axis=1, concat_axis=0, tiled=True),
        lax.all_to_all(values, "head", split_axis=1, concat_axis=0, tiled=True),
    )
    window = query_win.shape[0]
    groups = key_win.shape[1] // HD
    group = QH // KVH
    blocks = window // BLOCK
    width = doc_keys.shape[1]
    key_loc = key_win.reshape(window, groups, HD)
    value_loc = value_win.reshape(window, groups, HD)
    own_cites = lax.dynamic_slice_in_dim(citations, roll_index, 1, 0)[0]
    positions = jnp.arange(CITE, dtype=jnp.int32)
    listed = jnp.sum(
        jnp.where(block_lists[:, :, None] == positions[None, None, :], own_cites[None, None, :], 0),
        axis=-1,
    )
    pool_key, pool_value = (
        lax.all_gather(doc_keys, "roll", axis=0, tiled=True),
        lax.all_gather(doc_values, "roll", axis=0, tiled=True),
    )
    pool_key = pool_key.reshape(-1, BLOCK, width)
    pool_value = pool_value.reshape(-1, BLOCK, width)
    block_keys = pool_key[listed]
    block_values = pool_value[listed]
    query_blocks = query_win.reshape(blocks, BLOCK, groups, group, HD)
    grad_blocks = grad_win.reshape(blocks, BLOCK, groups, group, HD)
    outputs = []
    dqueries = []
    dkey_docs = []
    dvalue_docs = []
    key_acc = jnp.zeros((window, groups, HD), jnp.float32)
    value_acc = jnp.zeros((window, groups, HD), jnp.float32)
    for index_b in range(blocks):
        end = (index_b + 1) * BLOCK
        key_doc = block_keys[index_b].reshape(-1, groups, HD)
        value_doc = block_values[index_b].reshape(-1, groups, HD)
        output, dquery, dkey_loc, dvalue_loc, dkey_doc, dvalue_doc = block_pass(
            query_blocks[index_b],
            grad_blocks[index_b],
            key_loc[:end],
            value_loc[:end],
            key_doc,
            value_doc,
            index_b * BLOCK,
        )
        key_acc = key_acc.at[:end].add(dkey_loc)
        value_acc = value_acc.at[:end].add(dvalue_loc)
        outputs.append(output)
        dqueries.append(dquery)
        dkey_docs.append(dkey_doc)
        dvalue_docs.append(dvalue_doc)
    attended = jnp.stack(outputs).reshape(window, -1)
    query_grad = jnp.stack(dqueries).reshape(window, -1)
    key_grad = key_acc.astype(jnp.bfloat16).reshape(window, -1)
    value_grad = value_acc.astype(jnp.bfloat16).reshape(window, -1)
    flat_key = jnp.stack(dkey_docs).reshape(-1, BLOCK, width)
    flat_value = jnp.stack(dvalue_docs).reshape(-1, BLOCK, width)
    targets = listed.reshape(-1)
    pool_count = pool_key.shape[0]
    table = (targets[:, None] == jnp.arange(pool_count, dtype=jnp.int32)[None, :]).astype(
        jnp.float32
    )
    part_key = jnp.einsum("ns,ntc->stc", table, flat_key, precision=lax.Precision.HIGHEST)
    part_value = jnp.einsum("ns,ntc->stc", table, flat_value, precision=lax.Precision.HIGHEST)
    doc_key_grad, doc_value_grad = (
        lax.psum_scatter(
            part_key.reshape(-1, width).astype(jnp.bfloat16),
            "roll",
            scatter_dimension=0,
            tiled=True,
        ).astype(jnp.float32),
        lax.psum_scatter(
            part_value.reshape(-1, width).astype(jnp.bfloat16),
            "roll",
            scatter_dimension=0,
            tiled=True,
        ).astype(jnp.float32),
    )
    attended, query_grad, key_grad, value_grad = (
        lax.all_to_all(attended, "head", split_axis=0, concat_axis=1, tiled=True),
        lax.all_to_all(query_grad, "head", split_axis=0, concat_axis=1, tiled=True),
        lax.all_to_all(key_grad, "head", split_axis=0, concat_axis=1, tiled=True),
        lax.all_to_all(value_grad, "head", split_axis=0, concat_axis=1, tiled=True),
    )
    return (attended, query_grad, key_grad, value_grad, doc_key_grad, doc_value_grad)


def solution(mesh):
    return jax.shard_map(
        local,
        mesh=mesh,
        in_specs=(
            P(("roll", "head"), None),
            P(("roll", "head"), None),
            P(("roll", "head"), None),
            P(("roll", "head"), None),
            P("roll", "head"),
            P("roll", "head"),
            P(),
            P("roll", None),
        ),
        out_specs=(
            P(("roll", "head"), None),
            P(("roll", "head"), None),
            P(("roll", "head"), None),
            P(("roll", "head"), None),
            P("roll", "head"),
            P("roll", "head"),
        ),
        check_vma=False,
    )
```

profile of v0, /device:TPU:0, one launch (start us, length us, event | category | flops | bytes accessed | tf_op | source)
XLA Modules:
  0.0 658.5 jit_solution(9958374236072394001)
XLA Ops:
  8.7 4.2 all-to-all-start
  12.8 1.9 copy.269
  14.7 4.0 all-to-all-done
  18.7 3.5 all-to-all-start.1
  23.0 0.8 copy.268
  24.2 14.2 %all-to-all-done.1 = bf16[32,8,1024]{2,0,1:T(8,128)(2,1)S(1)} async-done(((bf16[32,8,1024]{2,0,1:T(8,128)(2,1)}), bf16[32,8,1024]{2,0,1:T(8,128)(2,1)S(1)}, u32[]{:S(2)}, u32[]{:S(2)}) %all-to-all-start.1) | async-done | bytes 524320 | tf_op jit(solution)/shard_map/all_to_all | solution.py:63
  38.4 3.5 all-to-all-start.4
  42.9 18.0 %all-to-all-done.4 = bf16[32,8,1024]{2,0,1:T(8,128)(2,1)S(1)} async-done(((bf16[32,8,1024]{2,0,1:T(8,128)(2,1)}), bf16[32,8,1024]{2,0,1:T(8,128)(2,1)S(1)}, u32[]{:S(2)}, u32[]{:S(2)}) %all-to-all-start.4) | async-done | bytes 524320 | tf_op jit(solution)/shard_map/all_to_all | solution.py:64
  60.9 0.8 copy.208
  61.7 0.8 copy.209
  62.5 1.0 fusion.104
  63.8 44.0 %all-gather.3.cloned.1.call-done = bf16[8192,128]{1,0:T(8,128)(2,1)} async-done(((bf16[256,128]{1,0:T(8,128)(2,1)}), bf16[8192,128]{1,0:T(8,128)(2,1)}) %all-gather.3.cloned.1.call-update) | async-done | bytes 2097168 | tf_op jit(solution)/shard_map/all_gather | solution.py:82
  107.9 2.2 gather_fusion
  110.7 1.4 bitcast_reduce_fusion
  115.4 1.9 convolution_convert_fusion
  117.4 2.7 copy.177
  120.1 0.9 copy_bitcast_fusion.4
  121.0 8.3 %all_to_all.140 = bf16[32,8,128]{2,0,1:T(8,128)(2,1)S(1)} all-to-all(bf16[32,8,128]{2,0,1:T(8,128)(2,1)S(1)} %copy_bitcast_fusion.4), channel_id=1, replica_groups=mesh['roll'=32,'head'=8] {'head'}, dimensions={1} | all-to-all | bytes 131072 | tf_op jit(solution)/shard_map/all_to_all | solution.py:66
  130.5 66.6 %all-gather.5.cloned.1.call-done = bf16[8192,128]{1,0:T(8,128)(2,1)} async-done(((bf16[256,128]{1,0:T(8,128)(2,1)}), bf16[8192,128]{1,0:T(8,128)(2,1)}) %all-gather.5.cloned.1.call-update) | async-done | bytes 2097168 | tf_op jit(solution)/shard_map/all_gather | solution.py:83
  197.0 3.0 gather_fusion.1
  200.0 1.4 convolution_bitcast_fusion.12
  201.4 1.0 fusion.35
  202.4 4.0 all-to-all-start.7
  206.6 1.0 fusion.101
  207.7 2.5 multiply_reduce_fusion
  211.2 1.0 multiply_reduce_fusion.1
  216.2 1.9 convolution_convert_fusion.1
  218.1 2.7 copy.173
  220.9 1.4 fusion.55
  222.5 1.3 convolution_bitcast_fusion.5
  224.3 0.8 copy-done.21
  226.1 1.1 copy-done.3
  228.1 0.9 fusion.34
  229.0 4.8 all-to-all-start.6
  234.2 1.0 all_to_all.113
  235.2 4.7 all-to-all-done.6
  240.0 3.7 all-to-all-start.3
  245.9 1.0 all_to_all.120
  246.9 14.8 %all-to-all-done.3 = bf16[8,32,1024]{2,1,0:T(8,128)(2,1)S(1)} async-done(((bf16[8,32,1024]{2,1,0:T(8,128)(2,1)}), bf16[8,32,1024]{2,1,0:T(8,128)(2,1)S(1)}, u32[]{:S(2)}, u32[]{:S(2)}) %all-to-all-start.3) | async-done | bytes 524320 | tf_op jit(solution)/shard_map/all_to_all | solution.py:144
  261.7 3.5 all-to-all-start.5
  265.2 1.5 copy_bitcast_fusion.2
  267.3 0.8 copy.202
  268.2 15.8 %all-to-all-done.5 = bf16[8,32,1024]{2,1,0:T(8,128)(2,1)S(1)} async-done(((bf16[8,32,1024]{2,1,0:T(8,128)(2,1)}), bf16[8,32,1024]{2,1,0:T(8,128)(2,1)S(1)}, u32[]{:S(2)}, u32[]{:S(2)}) %all-to-all-start.5) | async-done | bytes 524320 | tf_op jit(solution)/shard_map/all_to_all | solution.py:145
  283.9 0.8 copy.203
  284.8 138.9 %reduce-scatter.5.cloned.1.call-done = bf16[256,128]{1,0:T(8,128)(2,1)} async-done(((bf16[8192,128]{1,0:T(8,128)(2,1)}), bf16[256,128]{1,0:T(8,128)(2,1)}) %reduce-scatter.5.cloned.1.call-update) | async-done | bytes 65552 | tf_op jit(solution)/shard_map/reduce_scatter | solution.py:136
  423.7 1.5 convert_element_type.112
  425.2 225.3 %reduce-scatter.3.cloned.1.call-done = bf16[256,128]{1,0:T(8,128)(2,1)} async-done(((bf16[8192,128]{1,0:T(8,128)(2,1)}), bf16[256,128]{1,0:T(8,128)(2,1)}) %reduce-scatter.3.cloned.1.call-update) | async-done | bytes 65552 | tf_op jit(solution)/shard_map/reduce_scatter | solution.py:130
  650.5 1.5 convert_element_type.109
  (150 shorter events, 19.8 us)
Async XLA Ops:
  7.2 15.8 %copy-start.22 = (bf16[32,8192]{1,0:T(8,128)(2,1)S(1)}, bf16[32,8192]{1,0:T(8,128)(2,1)}, u32[]{:S(2)}) copy-start(bf16[32,8192]{1,0:T(8,128)(2,1)} %param.23) | copy-start | bytes 1572868
  7.2 16.7 %copy-start.41 = (s32[32,16]{0,1:T(8,128)S(1)}, s32[32,16]{0,1:T(8,128)}, u32[]{:S(2)}) copy-start(s32[32,16]{0,1:T(8,128)} %param.26) | copy-start | bytes 6148
  7.2 16.8 %copy-start.44 = (s32[2,4]{1,0:T(2,128)S(1)}, s32[2,4]{1,0:T(2,128)}, u32[]{:S(2)}) copy-start(s32[2,4]{1,0:T(2,128)} %param.27) | copy-start | bytes 100
  7.2 100.7 %all-gather.3.cloned.1.call-start = ((), (), s32[]{:S(2)}) async-start(), calls=%async_computation.10 | async-start | bytes 2162688 | tf_op jit(solution)/shard_map/all_gather | solution.py:82
  8.7 10.1 %all-to-all-start = ((bf16[32,8,128]{2,0,1:T(8,128)(2,1)}), bf16[32,8,128]{2,0,1:T(8,128)(2,1)S(1)}, u32[]{:S(2)}, u32[]{:S(2)}) async-start(bf16[32,8,128]{2,0,1:T(8,128)(2,1)} %copy_bitcast_fusion.5), calls=%async_computation | async-start | bytes 131072 | tf_op jit(solution)/shard_map/all_to_all | solution.py:65
  18.7 19.7 %all-to-all-start.1 = ((bf16[32,8,1024]{2,0,1:T(8,128)(2,1)}), bf16[32,8,1024]{2,0,1:T(8,128)(2,1)S(1)}, u32[]{:S(2)}, u32[]{:S(2)}) async-start(bf16[32,8,1024]{2,0,1:T(8,128)(2,1)} %bitcast.385), calls=%async_computation.1 | async-start | bytes 1048576 | tf_op jit(solution)/shard_map/all_to_all | solution.py:63
  22.2 174.8 %all-gather.5.cloned.1.call-start = ((), (), s32[]{:S(2)}) async-start(), calls=%async_computation.11 | async-start | bytes 2162688 | tf_op jit(solution)/shard_map/all_gather | solution.py:83
  38.4 22.5 %all-to-all-start.4 = ((bf16[32,8,1024]{2,0,1:T(8,128)(2,1)}), bf16[32,8,1024]{2,0,1:T(8,128)(2,1)S(1)}, u32[]{:S(2)}, u32[]{:S(2)}) async-start(bf16[32,8,1024]{2,0,1:T(8,128)(2,1)} %bitcast.384), calls=%async_computation.4 | async-start | bytes 1048576 | tf_op jit(solution)/shard_map/all_to_all | solution.py:64
  41.9 381.7 %reduce-scatter.5.cloned.1.call-start = ((), (), s32[]{:S(2)}) async-start(), calls=%async_computation.13 | async-start | bytes 2162688 | tf_op jit(solution)/shard_map/reduce_scatter | solution.py:136
  42.7 65.2 %copy-start.40 = (s32[1024]{0:T(1024)}, s32[1024]{0:T(1024)S(1)}, u32[]{:S(2)}) copy-start(s32[1024]{0:T(1024)S(1)} %pad_clamp_fusion) | copy-start | bytes 12292
  42.8 19.7 %copy-start.23 = (bf16[4,32,128]{2,1,0:T(8,128)(2,1)}, bf16[4,32,128]{2,1,0:T(8,128)(2,1)S(1)}, u32[]{:S(2)}) copy-start(bf16[4,32,128]{2,1,0:T(8,128)(2,1)S(1)} %slice.134) | copy-start | bytes 98308
  42.9 20.9 %copy-start.10 = (bf16[16,8,8,128]{3,2,1,0:T(8,128)(2,1)}, bf16[16,8,8,128]{3,2,1,0:T(8,128)(2,1)S(1)}, u32[]{:S(2)}) copy-start(bf16[16,8,8,128]{3,2,1,0:T(8,128)(2,1)S(1)} %copy.207) | copy-start | bytes 786436
  110.1 2.6 copy-start.17
  112.3 1.0 copy-start.8
  112.7 1.1 copy-start.27
  113.2 1.3 copy-start.1
  200.0 1.4 copy-start.28
  202.4 26.6 %all-to-all-start.7 = ((bf16[8,32,128]{2,1,0:T(8,128)(2,1)}), bf16[8,32,128]{2,1,0:T(8,128)(2,1)}, u32[]{:S(2)}, u32[]{:S(2)}) async-start(bf16[8,32,128]{2,1,0:T(8,128)(2,1)} %bitcast.434), calls=%async_computation.7 | async-start | bytes 131072 | tf_op jit(solution)/shard_map/all_to_all | solution.py:147
  206.4 444.1 %reduce-scatter.3.cloned.1.call-start = ((), (), s32[]{:S(2)}) async-start(), calls=%async_computation.12 | async-start | bytes 2162688 | tf_op jit(solution)/shard_map/reduce_scatter | solution.py:130
  207.6 2.5 copy-start.34
  207.6 4.6 copy-start.32
  207.6 2.5 copy-start.29
  210.1 1.0 copy-start.9
  210.1 1.1 copy-start.26
  210.1 1.1 copy-start.39
  210.7 1.7 copy-start.2
  210.8 2.3 copy-start.36
  213.0 2.0 copy-start.38
  214.0 1.0 copy-start.6
  215.6 2.5 copy-start.4
  220.9 3.0 copy-start.31
  222.3 2.0 copy-start.13
  223.9 1.2 copy-start.21
  223.9 1.2 copy-start.37
  224.3 1.1 copy-start.35
  225.4 2.5 copy-start.15
  225.4 1.8 copy-start.3
  225.4 1.8 copy-start.33
  229.0 10.9 %all-to-all-start.6 = ((bf16[8,32,128]{2,1,0:T(8,128)(2,1)}), bf16[8,32,128]{2,1,0:T(8,128)(2,1)S(1)}, u32[]{:S(2)}, u32[]{:S(2)}) async-start(bf16[8,32,128]{2,1,0:T(8,128)(2,1)} %bitcast.89), calls=%async_computation.6 | async-start | bytes 131072 | tf_op jit(solution)/shard_map/all_to_all | solution.py:146
  233.8 9.9 %copy-start.16 = (bf16[8,128,256]{1,2,0:T(8,128)(2,1)S(1)}, bf16[8,128,256]{1,2,0:T(8,128)(2,1)}, u32[]{:S(2)}) copy-start(bf16[8,128,256]{1,2,0:T(8,128)(2,1)} %copy-done.15) | copy-start | bytes 1572868
  233.9 10.2 %copy-start.7 = (bf16[8,128,512]{1,2,0:T(8,128)(2,1)S(1)}, bf16[8,128,512]{1,2,0:T(8,128)(2,1)}, u32[]{:S(2)}) copy-start(bf16[8,128,512]{1,2,0:T(8,128)(2,1)} %copy-done.6) | copy-start | bytes 3145732
  233.9 10.2 %copy-start.20 = (bf16[4,128,128]{2,1,0:T(8,128)(2,1)S(1)}, bf16[4,128,128]{2,1,0:T(8,128)(2,1)}, u32[]{:S(2)}) copy-start(bf16[4,128,128]{2,1,0:T(8,128)(2,1)} %copy-done.19) | copy-start | bytes 393220
  235.2 9.4 %copy-start.14 = (bf16[8,128,128]{1,2,0:T(8,128)(2,1)S(1)}, bf16[8,128,128]{1,2,0:T(8,128)(2,1)}, u32[]{:S(2)}) copy-start(bf16[8,128,128]{1,2,0:T(8,128)(2,1)} %copy-done.13) | copy-start | bytes 786436
  235.2 9.4 %copy-start.24 = (bf16[4,32,128]{2,1,0:T(8,128)(2,1)S(1)}, bf16[4,32,128]{2,1,0:T(8,128)(2,1)}, u32[]{:S(2)}) copy-start(bf16[4,32,128]{2,1,0:T(8,128)(2,1)} %copy-done.23) | copy-start | bytes 98308
  240.0 21.8 %all-to-all-start.3 = ((bf16[8,32,1024]{2,1,0:T(8,128)(2,1)}), bf16[8,32,1024]{2,1,0:T(8,128)(2,1)S(1)}, u32[]{:S(2)}, u32[]{:S(2)}) async-start(bf16[8,32,1024]{2,1,0:T(8,128)(2,1)} %all_to_all.113), calls=%async_computation.3 | async-start | bytes 1048576 | tf_op jit(solution)/shard_map/all_to_all | solution.py:144
  243.7 1.2 copy-start.5
  243.7 1.2 copy-start.18
  261.7 22.2 %all-to-all-start.5 = ((bf16[8,32,1024]{2,1,0:T(8,128)(2,1)}), bf16[8,32,1024]{2,1,0:T(8,128)(2,1)S(1)}, u32[]{:S(2)}, u32[]{:S(2)}) async-start(bf16[8,32,1024]{2,1,0:T(8,128)(2,1)} %all_to_all.120), calls=%async_computation.5 | async-start | bytes 1048576 | tf_op jit(solution)/shard_map/all_to_all | solution.py:145
  (8 other events, 6.2 us)
Sparse Core Ops, SparseCore 0:
  11.6 96.2 all-gather.2
  111.4 85.6 all-gather.4
  199.6 224.0 reduce-scatter.4
  426.2 224.2 reduce-scatter.2
where the time goes:
time: 660 us; the launch traced here: 659 us
  waiting for transfers between devices  548 us (83%)
  local copies, waits for them, and re-layouts  31.2 us (5%)
  starting transfers between devices  27.4 us (4%)
  matrix products  21.9 us (3%)
  between operations  14.6 us (2%)
  blocking collectives  8.3 us (1%)
  other arithmetic  7.31 us (1%)
    reduce_scatter x1, waiting for transfers between devices, local(): lax.psum_scatter(part_key.reshape(-1, width).astype(jnp.bfloat16), 'roll'...  225 us
    reduce_scatter x1, waiting for transfers between devices, local(): lax.psum_scatter(part_value.reshape(-1, width).astype(jnp.bfloat16), 'rol...  139 us
    all_gather x1, waiting for transfers between devices, local(): lax.all_gather(doc_values, 'roll', axis=0, tiled=True)  66.6 us
    all_gather x1, waiting for transfers between devices, local(): lax.all_gather(doc_keys, 'roll', axis=0, tiled=True)  44 us
    all_to_all x1, waiting for transfers between devices, local(): lax.all_to_all(cotangent, 'head', split_axis=1, concat_axis=0, tiled=True)  18 us
    all_to_all x1, waiting for transfers between devices, local(): lax.all_to_all(query_grad, 'head', split_axis=0, concat_axis=1, tiled=True)  15.8 us
    all_to_all x1, waiting for transfers between devices, local(): lax.all_to_all(attended, 'head', split_axis=0, concat_axis=1, tiled=True)  14.8 us
    all_to_all x1, waiting for transfers between devices, local(): lax.all_to_all(queries, 'head', split_axis=1, concat_axis=0, tiled=True)  14.2 us
  transfers between devices with their start and end apart: 11, of which 10 were waited for; matrix products, arithmetic and copies ran while one was open for 8% of the time, Pallas kernels for 0%

commit v1 on v0

v1 whole, which is shorter than its diff:
```python
import functools
import math

import jax
import jax.numpy as jnp
from jax import lax
from jax.experimental import pallas as pl
from jax.experimental.pallas import tpu as pltpu
from jax.sharding import PartitionSpec as P

HD = 128
BLOCK = 128
GROUP = 8
LIST = 4
QTOK = 256
NX = 4
NY = 4
NH = 8
WIDE = GROUP * HD
ROWS = QTOK // NH
KEYS = LIST * BLOCK + QTOK
NONE = KEYS // BLOCK
MESH = pl.DeviceIdType.MESH
SCALE = 1.0 / math.sqrt(HD)
LOG2E = math.log2(math.e)
F32 = jnp.float32
BF16 = jnp.bfloat16


def roll_of(x, y, z):
    return (y * 2 + z) * NX + x


def dot(a, b, ca, cb):
    return lax.dot_general(a, b, (((ca,), (cb,)), ((), ())), preferred_element_type=F32)


def kernel(
    q_ref, g_ref, k_ref, v_ref, dk_ref, dv_ref, par_ref, slot_ref, pos_ref,
    att_ref, qg_ref, kg_ref, vg_ref, dkg_ref, dvg_ref,
    qw, gw, kw, vw, ag, sel, pool, cat, cat_t, acc, att, dq, kv_out, gs, gr, s1, r1, zs, zr,
    own_q, own_doc, head_s, head_r, z_s, z_r, one_s, one_r, two_s, two_r,
    out_s, out_r, out_l, two_bs, two_br, one_bs, one_br, zb_s, zb_r,
):
    roll = lax.axis_index("roll")
    head = lax.axis_index("head")
    x = lax.rem(roll, NX)
    zh = lax.rem(roll // NX, 2)
    y = roll // (2 * NX)
    z_dev = (roll_of(x, y, 1 - zh), head)

    place = (x, y)
    size = (NX, NY)
    docs = (dk_ref, dv_ref)

    def at(t, a, b, z):
        return roll_of(a, b, z) if t == 0 else roll_of(b, a, z)

    def first(t, d):
        a = lax.rem(place[t] + d, size[t])
        return (at(t, a, place[1 - t], zh), head)

    def second(t, d):
        b = lax.rem(place[1 - t] + d, size[1 - t])
        return (at(t, place[t], b, zh), head)

    def remote(src, dst, ss, rs, dev):
        return pltpu.make_async_remote_copy(
            src_ref=src, dst_ref=dst, send_sem=ss, recv_sem=rs, device_id=dev, device_id_type=MESH
        )

    barrier = pltpu.get_barrier_semaphore()
    partners = [z_dev]
    partners += [first(t, d) for t in range(2) for d in range(1, size[t])]
    partners += [(roll, lax.rem(head + k, NH)) for k in range(1, NH)]
    for dev in partners:
        pl.semaphore_signal(barrier, inc=1, device_id=dev, device_id_type=MESH)
    pl.semaphore_wait(barrier, len(partners))

    z_copy = []
    for t in range(2):
        c = remote(docs[t], ag.at[t, 1, place[t]], z_s.at[t], z_r.at[t], z_dev)
        c.start()
        z_copy.append(c)
    one = [[[], []], [[], []]]
    for t in range(2):
        for d in range(1, size[t]):
            c = remote(
                docs[t], ag.at[t, 0, place[t]], one_s.at[t, 0, d], one_r.at[t, 0, d], first(t, d)
            )
            c.start()
            one[t][0].append(c)
    own_docs = []
    for t in range(2):
        c = pltpu.make_async_copy(docs[t], ag.at[t, 0, place[t]], own_doc.at[t])
        c.start()
        own_docs.append(c)
    heads = []
    mine = pl.ds(pl.multiple_of(head * ROWS, ROWS), ROWS)
    for i, (src, dst, width) in enumerate(
        ((k_ref, kw, HD), (v_ref, vw, HD), (q_ref, qw, WIDE), (g_ref, gw, WIDE))
    ):
        c = pltpu.make_async_copy(
            src.at[:, pl.ds(pl.multiple_of(head * width, width), width)], dst.at[mine], own_q.at[i]
        )
        c.start()
        heads.append(c)
    sends = []
    for k in range(1, NH):
        h = lax.rem(head + k, NH)
        for i, (src, dst, width) in enumerate(
            ((k_ref, kw, HD), (v_ref, vw, HD), (q_ref, qw, WIDE), (g_ref, gw, WIDE))
        ):
            c = remote(
                src.at[:, pl.ds(pl.multiple_of(h * width, width), width)],
                dst.at[mine], head_s.at[k, i], head_r.at[k, i], (roll, h),
            )
            c.start()
            sends.append(c)

    acc[...] = jnp.zeros_like(acc)

    def slot(t, p, b, a):
        return (p * size[1 - t] + b) * size[t] + a

    def pick(t, p):
        o_z = zh if p == 0 else 1 - zh
        for d in range(size[1 - t]):
            target = second(t, d)[0]

            def step(a, _):
                pr = par_ref[target, at(t, a, place[1 - t], o_z)]
                low = ag[t, p, a, 0:BLOCK].astype(F32)
                high = ag[t, p, a, BLOCK : 2 * BLOCK].astype(F32)
                chosen = (low * (1.0 - pr) + high * pr).astype(BF16)
                if d == 0:
                    pool[t, slot(t, p, place[1 - t], a)] = chosen
                else:
                    sel[t, p, d - 1, a] = chosen
                return 0

            lax.fori_loop(0, size[t], step, 0)

    two = []
    for p in range(2):
        if p == 1:
            for t in range(2):
                z_copy[t].wait_recv()
                for d in range(1, size[t]):
                    c = remote(
                        ag.at[t, 1, place[t]], ag.at[t, 1, place[t]],
                        one_s.at[t, 1, d], one_r.at[t, 1, d], first(t, d),
                    )
                    c.start()
                    one[t][1].append(c)
        for t in range(2):
            if p == 0:
                own_docs[t].wait()
            for c in one[t][p]:
                c.wait_recv()
            pick(t, p)
            for d in range(1, size[1 - t]):
                c = remote(
                    sel.at[t, p, d - 1], pool.at[t, pl.ds(slot(t, p, place[1 - t], 0), size[t])],
                    two_s.at[t, p, d], two_r.at[t, p, d], second(t, d),
                )
                c.start()
                two.append(c)
    for c in heads:
        c.wait()
    for c in sends:
        c.wait_recv()
    for c in two:
        c.wait_recv()

    for b in range(2):
        for i in range(LIST):
            rows = pl.ds(i * BLOCK, BLOCK)
            for t in range(2):
                cat[t, b, rows] = pool[t, slot_ref[t, b * LIST + i]]
        cat[0, b, LIST * BLOCK : KEYS] = kw[...]
        cat[1, b, LIST * BLOCK : KEYS] = vw[...]
        for t in range(2):
            cat_t[t, b] = cat[t, b].T

    def compute(step, _):
        b = step // (GROUP // 2)
        c0 = pl.multiple_of(lax.rem(step, GROUP // 2) * 2 * HD, 2 * HD)
        c1 = pl.multiple_of(c0 + HD, HD)
        rows = pl.ds(pl.multiple_of(b * BLOCK, BLOCK), BLOCK)
        cols = (pl.ds(c0, HD), pl.ds(c1, HD))
        query = jnp.concatenate([qw[rows, c] for c in cols], axis=0)
        grad = jnp.concatenate([gw[rows, c] for c in cols], axis=0)
        score = dot(cat[0, b], query, 1, 1)
        local = score[LIST * BLOCK :]
        key_at = lax.broadcasted_iota(jnp.int32, local.shape, 0)
        query_at = lax.rem(lax.broadcasted_iota(jnp.int32, local.shape, 1), BLOCK) + b * BLOCK
        local = jnp.where(key_at <= query_at, local, -jnp.inf)
        score = jnp.concatenate([score[: LIST * BLOCK], local], axis=0)
        top = jnp.max(score, axis=0, keepdims=True)
        e = jnp.exp2((score - top) * (SCALE * LOG2E))
        prob = e * (1.0 / jnp.sum(e, axis=0, keepdims=True))
        weight = prob.astype(BF16)
        dprob = dot(cat[1, b], grad, 1, 1)
        delta = jnp.sum(prob * dprob, axis=0, keepdims=True)
        dscore = (prob * (dprob - delta)).astype(BF16)
        acc[1, b, 0:NONE] += dot(weight, grad, 1, 0).reshape(NONE, BLOCK, HD)
        acc[0, b, 0:NONE] += dot(dscore, query, 1, 0).reshape(NONE, BLOCK, HD)
        out_t = dot(cat_t[1, b], weight, 1, 0)
        dq_t = dot(cat_t[0, b], dscore, 1, 0) * SCALE
        for i, c in enumerate(cols):
            att[rows, c] = out_t[:, i * HD : (i + 1) * HD].T.astype(BF16)
            dq[rows, c] = dq_t[:, i * HD : (i + 1) * HD].T.astype(BF16)
        return 0

    lax.fori_loop(0, GROUP, compute, 0)

    def prepare(t, p):
        def step(n, _):
            b, a = n // size[t], lax.rem(n, size[t])
            m = p * size[0] * size[1] + n
            total = acc[t, 0, pos_ref[t, 0, m]] + acc[t, 1, pos_ref[t, 1, m]]
            if t == 0:
                total = total * SCALE
            gs[t, p, b, a] = total.astype(BF16)
            return 0

        lax.fori_loop(0, size[0] * size[1], step, 0)
        b = place[1 - t]
        gr[t, p, b] = gs[t, p, b]

    back_two = [[[], []], [[], []]]
    for p in (1, 0):
        for t in range(2):
            prepare(t, p)
            for d in range(1, size[1 - t]):
                b = lax.rem(place[1 - t] + d, size[1 - t])
                c = remote(
                    gs.at[t, p, b], gr.at[t, p, place[1 - t]],
                    two_bs.at[t, p, d], two_br.at[t, p, d], second(t, d),
                )
                c.start()
                back_two[t][p].append(c)

    for t in range(2):
        total = (acc[t, 0, LIST:NONE] + acc[t, 1, LIST:NONE]).reshape(QTOK, HD)
        if t == 0:
            total = total * SCALE
        kv_out[t] = total.astype(BF16)

    outs = []
    back = (
        (kv_out.at[0], kg_ref, HD), (kv_out.at[1], vg_ref, HD), (att, att_ref, WIDE), (dq, qg_ref, WIDE)
    )
    local_outs = []
    for i, (src, dst, width) in enumerate(back):
        there = pl.ds(pl.multiple_of(head * width, width), width)
        c = pltpu.make_async_copy(src.at[mine], dst.at[:, there], out_l.at[i])
        c.start()
        local_outs.append(c)
        for k in range(1, NH):
            h = lax.rem(head + k, NH)
            theirs = pl.ds(pl.multiple_of(h * ROWS, ROWS), ROWS)
            c = remote(
                src.at[theirs], dst.at[:, there], out_s.at[k, i], out_r.at[k, i], (roll, h)
            )
            c.start()
            outs.append(c)

    back_one = [[[], []], [[], []]]
    back_z = [None, None]
    kept = [None, None]
    for p in (1, 0):
        o_z = zh if p == 0 else 1 - zh
        for t in range(2):
            for c in back_two[t][p]:
                c.wait_recv()

            def merge(a, _):
                o = at(t, a, place[1 - t], o_z)
                low = high = jnp.zeros((BLOCK, HD), F32)
                for b in range(size[1 - t]):
                    pr = par_ref[at(t, place[t], b, zh), o]
                    m = gr[t, p, b, a].astype(F32)
                    low = low + m * (1.0 - pr)
                    high = high + m * pr
                s1[t, p, a, 0:BLOCK] = low.astype(BF16)
                s1[t, p, a, BLOCK : 2 * BLOCK] = high.astype(BF16)
                return 0

            lax.fori_loop(0, size[t], merge, 0)
            for d in range(1, size[t]):
                a = lax.rem(place[t] + d, size[t])
                c = remote(
                    s1.at[t, p, a], r1.at[t, p, place[t]],
                    one_bs.at[t, p, d], one_br.at[t, p, d], first(t, d),
                )
                c.start()
                back_one[t][p].append(c)
            r1[t, p, place[t]] = s1[t, p, place[t]]
    for p in (1, 0):
        for t in range(2):
            for c in back_one[t][p]:
                c.wait_recv()
            total = r1[t, p, 0].astype(F32)
            for a in range(1, size[t]):
                total = total + r1[t, p, a].astype(F32)
            if p == 1:
                zs[t] = total.astype(BF16)
                c = remote(zs.at[t], zr.at[t], zb_s.at[t], zb_r.at[t], z_dev)
                c.start()
                back_z[t] = c
            else:
                kept[t] = total
    for t, ref in enumerate((dkg_ref, dvg_ref)):
        back_z[t].wait_recv()
        ref[...] = kept[t] + zr[t].astype(F32)

    for c in local_outs:
        c.wait()
    for c in outs:
        c.wait_recv()
    for c in z_copy + sends + two + outs + back_z:
        c.wait_send()
    for group in (one, back_two, back_one):
        for t in range(2):
            for p in range(2):
                for c in group[t][p]:
                    c.wait_send()


def local(queries, keys, values, cotangent, doc_keys, doc_values, citations, block_lists):
    rolls = 2 * NX * NY
    roll = lax.axis_index("roll")
    zh = (roll // NX) % 2
    owner = jnp.arange(rolls, dtype=jnp.int32)
    par = jnp.sum(
        jnp.where(citations[:, None, :] // 2 == owner[None, :, None], citations[:, None, :] % 2, 0),
        axis=-1,
    ).astype(F32)
    own = lax.dynamic_slice_in_dim(citations, roll, 1, 0)[0]
    wanted = jnp.sum(
        jnp.where(
            block_lists[:, :, None] == jnp.arange(own.shape[0], dtype=jnp.int32), own[None, None, :], 0
        ),
        axis=-1,
    ) // 2
    plane = (wanted // NX) % 2 ^ zh
    wx, wy = wanted % NX, wanted // (2 * NX)
    slots = jnp.stack([(plane * NY + wy) * NX + wx, (plane * NX + wx) * NY + wy])
    pos = NONE + jnp.sum(
        jnp.where(
            slots[:, :, :, None] == owner,
            jnp.arange(LIST, dtype=jnp.int32)[None, None, :, None] - NONE,
            0,
        ),
        axis=2,
    )
    slots = slots.reshape(2, 2 * LIST)
    n = max(NX, NY)
    any_spec = pl.BlockSpec(memory_space=pltpu.HBM)
    vmem = pl.BlockSpec(memory_space=pltpu.VMEM)
    smem = pl.BlockSpec(memory_space=pltpu.SMEM)
    dma = pltpu.SemaphoreType.DMA
    blk = (BLOCK, HD)
    sd = jax.ShapeDtypeStruct
    return pl.pallas_call(
        kernel,
        out_shape=(
            sd(queries.shape, BF16), sd(queries.shape, BF16), sd(keys.shape, BF16), sd(keys.shape, BF16),
            sd(doc_keys.shape, F32), sd(doc_keys.shape, F32),
        ),
        in_specs=[any_spec] * 6 + [smem] * 3,
        out_specs=(any_spec,) * 4 + (vmem,) * 2,
        scratch_shapes=[
            pltpu.VMEM((QTOK, WIDE), BF16),
            pltpu.VMEM((QTOK, WIDE), BF16),
            pltpu.VMEM((QTOK, HD), BF16),
            pltpu.VMEM((QTOK, HD), BF16),
            pltpu.VMEM((2, 2, n, 2 * BLOCK, HD), BF16),
            pltpu.VMEM((2, 2, n - 1, n) + blk, BF16),
            pltpu.VMEM((2, 2 * n * n) + blk, BF16),
            pltpu.VMEM((2, 2, KEYS, HD), BF16),
            pltpu.VMEM((2, 2, HD, KEYS), BF16),
            pltpu.VMEM((2, 2, NONE + 1) + blk, F32),
            pltpu.VMEM((QTOK, WIDE), BF16),
            pltpu.VMEM((QTOK, WIDE), BF16),
            pltpu.VMEM((2, QTOK, HD), BF16),
            pltpu.VMEM((2, 2, n, n) + blk, BF16),
            pltpu.VMEM((2, 2, n, n) + blk, BF16),
            pltpu.VMEM((2, 2, n, 2 * BLOCK, HD), BF16),
            pltpu.VMEM((2, 2, n, 2 * BLOCK, HD), BF16),
            pltpu.VMEM((2, 2 * BLOCK, HD), BF16),
            pltpu.VMEM((2, 2 * BLOCK, HD), BF16),
            dma((4,)), dma((2,)), dma((NH, 4)), dma((NH, 4)), dma((2,)), dma((2,)),
            dma((2, 2, n)), dma((2, 2, n)), dma((2, 2, n)), dma((2, 2, n)),
            dma((NH, 4)), dma((NH, 4)), dma((4,)),
            dma((2, 2, n)), dma((2, 2, n)), dma((2, 2, n)), dma((2, 2, n)), dma((2,)), dma((2,)),
        ],
        compiler_params=pltpu.CompilerParams(
            collective_id=0, has_side_effects=True, vmem_limit_bytes=48 * 2**20
        ),
        name="attention",
    )(queries, cotangent, keys, values, doc_keys, doc_values, par, slots, pos)


def solution(mesh):
    return jax.shard_map(
        local,
        mesh=mesh,
        in_specs=(
            P(("roll", "head"), None),
            P(("roll", "head"), None),
            P(("roll", "head"), None),
            P(("roll", "head"), None),
            P("roll", "head"),
            P("roll", "head"),
            P(),
            P("roll", None),
        ),
        out_specs=(
            P(("roll", "head"), None),
            P(("roll", "head"), None),
            P(("roll", "head"), None),
            P(("roll", "head"), None),
            P("roll", "head"),
            P("roll", "head"),
        ),
        check_vma=False,
    )
```

time: 660 us -> 90.6 us (0.14)
  the two profiles are of different devices: /device:TPU:0 before, /device:TPU:33 now
where the time goes in v1:
time: 90.6 us; the launch traced here: 90.3 us
  Pallas kernels  81.1 us (90%)
  local copies, waits for them, and re-layouts  7.79 us (9%)
    pallas_call x1, Pallas kernels, local(): pl.pallas_call(kernel, out_shape=(sd(queries.shape, BF16), sd(queries.sha...  81.1 us
    unnamed x22, local copies, waits for them, and re-layouts  7.38 us

profile of v1, /device:TPU:33, one launch (start us, length us, event | category | flops | bytes accessed | tf_op | source)
XLA Modules:
  0.0 90.3 jit_solution(11444194260479526335)
XLA Ops:
  0.6 0.0 copy-start.7
  0.6 0.0 copy-start.6
  0.7 0.0 copy-start.5
  0.7 0.7 copy-done.6
  1.3 0.2 dynamic-slice_reduce_fusion
  1.5 0.0 copy-done.7
  1.5 0.2 select_reduce_fusion.2
  1.7 0.0 copy-start.4
  1.8 0.1 reduce_sum.33
  1.9 0.1 select_reduce_fusion.1
  2.1 0.0 copy-start.3
  2.1 0.0 copy-start.2
  2.1 0.1 copy.18
  2.2 0.1 copy.19
  2.2 0.2 select_reduce_fusion
  2.5 0.0 copy-done.5
  2.5 0.1 copy-done.4
  2.6 0.3 copy-done.3
  2.9 0.0 copy-done.2
  2.9 0.0 copy-start
  2.9 1.0 %copy-done = bf16[32,8192]{1,0:T(8,128)(2,1)S(1)} copy-done((bf16[32,8192]{1,0:T(8,128)(2,1)S(1)}, bf16[32,8192]{1,0:T(8,128)(2,1)}, u32[]{:S(2)}) %copy-start) | copy-done | bytes 524312
  4.0 0.0 copy-start.1
  4.0 1.0 %copy-done.1 = bf16[32,8192]{1,0:T(8,128)(2,1)S(1)} copy-done((bf16[32,8192]{1,0:T(8,128)(2,1)S(1)}, bf16[32,8192]{1,0:T(8,128)(2,1)}, u32[]{:S(2)}) %copy-start.1) | copy-done | bytes 524312
  5.0 81.1 %attention.1 = (bf16[32,8192]{1,0:T(8,128)(2,1)S(1)}, bf16[32,8192]{1,0:T(8,128)(2,1)S(1)}, bf16[32,1024]{1,0:T(8,128)(2,1)S(1)}, bf16[32,1024]{1,0:T(8,128)(2,1...) custom-call(bf16[32,8192]{1,0:T(8,128)(2,1)S(1)} %copy-done, bf16[32,8192]{1,0:T(8,128)(2,1)S(1)} %copy-done.1, ...), custom_call_target="tpu_custom_call" | custom-call | tf_op jit(solution)/shard_map/attention/pallas_call | solution.py:367
  86.1 0.8 copy.26
  86.9 0.8 copy.27
  87.7 0.6 copy.28
  88.4 0.6 copy.29
  89.0 0.7 copy.30
  89.7 0.7 copy.31
  (9 shorter events, 0.1 us)
Async XLA Ops:
  0.6 0.9 copy-start.7
  0.6 0.7 copy-start.6
  0.7 1.8 %copy-start.5 = (bf16[256,128]{1,0:T(8,128)(2,1)S(1)}, bf16[256,128]{1,0:T(8,128)(2,1)}, u32[]{:S(2)}) copy-start(bf16[256,128]{1,0:T(8,128)(2,1)} %dv_ref.1) | copy-start | bytes 196612
  1.7 0.8 copy-start.4
  2.1 0.8 copy-start.3
  2.1 0.9 copy-start.2
  2.9 1.0 %copy-start = (bf16[32,8192]{1,0:T(8,128)(2,1)S(1)}, bf16[32,8192]{1,0:T(8,128)(2,1)}, u32[]{:S(2)}) copy-start(bf16[32,8192]{1,0:T(8,128)(2,1)} %q_ref.1) | copy-start | bytes 1572868
  4.0 1.0 %copy-start.1 = (bf16[32,8192]{1,0:T(8,128)(2,1)S(1)}, bf16[32,8192]{1,0:T(8,128)(2,1)}, u32[]{:S(2)}) copy-start(bf16[32,8192]{1,0:T(8,128)(2,1)} %g_ref.1) | copy-start | bytes 1572868

commit v2 on v1

--- a/solution.py
+++ b/solution.py
@@ -20,6 +20,8 @@
 ROWS = QTOK // NH
 KEYS = LIST * BLOCK + QTOK
 NONE = KEYS // BLOCK
+PAIR = 2 * HD
+STEPS = GROUP // 2
 MESH = pl.DeviceIdType.MESH
 SCALE = 1.0 / math.sqrt(HD)
 LOG2E = math.log2(math.e)
@@ -36,11 +38,11 @@
 
 
 def kernel(
-    q_ref, g_ref, k_ref, v_ref, dk_ref, dv_ref, par_ref, slot_ref, pos_ref,
+    q_ref, g_ref, k_ref, v_ref, dk_ref, dv_ref, cite_v_ref, cite_ref, list_ref,
     att_ref, qg_ref, kg_ref, vg_ref, dkg_ref, dvg_ref,
     qw, gw, kw, vw, ag, sel, pool, cat, cat_t, acc, att, dq, kv_out, gs, gr, s1, r1, zs, zr,
-    own_q, own_doc, head_s, head_r, z_s, z_r, one_s, one_r, two_s, two_r,
-    out_s, out_r, out_l, two_bs, two_br, one_bs, one_br, zb_s, zb_r,
+    par_v, par_ref, par_sem, own_q, own_doc, kv_s, kv_r, head_s, head_r, z_s, z_r, one_s, one_r, two_s, two_r,
+    kvo_s, kvo_r, out_s, out_r, out_l, two_bs, two_br, one_bs, one_br, zb_s, zb_r,
 ):
     roll = lax.axis_index("roll")
     head = lax.axis_index("head")
@@ -69,6 +71,16 @@
             src_ref=src, dst_ref=dst, send_sem=ss, recv_sem=rs, device_id=dev, device_id_type=MESH
         )
 
+    acc[...] = jnp.zeros_like(acc)
+
+    cites = cite_v_ref[...]
+    rolls = 2 * NX * NY
+    owner_at = lax.broadcasted_iota(jnp.int32, (rolls, HD), 1)
+    odd = jnp.zeros((rolls, HD), jnp.int32)
+    for c in range(cites.shape[1]):
+        cite = cites[:, c : c + 1]
+        odd = odd + jnp.where((cite >> 1) == owner_at, cite & 1, 0)
+
     barrier = pltpu.get_barrier_semaphore()
     partners = [z_dev]
     partners += [first(t, d) for t in range(2) for d in range(1, size[t])]
@@ -76,6 +88,9 @@
     for dev in partners:
         pl.semaphore_signal(barrier, inc=1, device_id=dev, device_id_type=MESH)
     pl.semaphore_wait(barrier, len(partners))
+
+    par_v[...] = odd.astype(F32)
+    par_copy = pltpu.make_async_copy(par_v, par_ref, par_sem.at[0])
 
     z_copy = []
     for t in range(2):
@@ -95,30 +110,47 @@
         c = pltpu.make_async_copy(docs[t], ag.at[t, 0, place[t]], own_doc.at[t])
         c.start()
         own_docs.append(c)
+    par_copy.start()
     heads = []
     mine = pl.ds(pl.multiple_of(head * ROWS, ROWS), ROWS)
-    for i, (src, dst, width) in enumerate(
-        ((k_ref, kw, HD), (v_ref, vw, HD), (q_ref, qw, WIDE), (g_ref, gw, WIDE))
-    ):
+    moved = ((k_ref, kw, HD), (v_ref, vw, HD), (q_ref, qw, WIDE), (g_ref, gw, WIDE))
+    for i, (src, dst, width) in enumerate(moved):
         c = pltpu.make_async_copy(
             src.at[:, pl.ds(pl.multiple_of(head * width, width), width)], dst.at[mine], own_q.at[i]
         )
         c.start()
         heads.append(c)
-    sends = []
+
+    def kv_copy(k, i):
+        h = lax.rem(head + k, NH)
+        src, dst, width = moved[i]
+        return remote(
+            src.at[:, pl.ds(pl.multiple_of(h * width, width), width)],
+            dst.at[mine], kv_s.at[k, i], kv_r.at[k, i], (roll, h),
+        )
+
+    def chunk_copy(k, i, j):
+        h = lax.rem(head + k, NH)
+        src, dst, width = moved[2 + i]
+        return remote(
+            src.at[:, pl.ds(pl.multiple_of(h * width + j * PAIR, PAIR), PAIR)],
+            dst.at[mine, pl.ds(pl.multiple_of(j * PAIR, PAIR), PAIR)],
+            head_s.at[k, i, j], head_r.at[k, i, j], (roll, h),
+        )
+
     for k in range(1, NH):
-        h = lax.rem(head + k, NH)
-        for i, (src, dst, width) in enumerate(
-            ((k_ref, kw, HD), (v_ref, vw, HD), (q_ref, qw, WIDE), (g_ref, gw, WIDE))
-        ):
-            c = remote(
-                src.at[:, pl.ds(pl.multiple_of(h * width, width), width)],
-                dst.at[mine], head_s.at[k, i], head_r.at[k, i], (roll, h),
-            )
-            c.start()
-            sends.append(c)
-
-    acc[...] = jnp.zeros_like(acc)
+        for i in range(2):
+            kv_copy(k, i).start()
+
+    def send_chunks(j, _):
+        for k in range(1, NH):
+            for i in range(2):
+                chunk_copy(k, i, j).start()
+        return 0
+
+    lax.fori_loop(0, STEPS, send_chunks, 0)
+
+    par_copy.wait()
 
     def slot(t, p, b, a):
         return (p * size[1 - t] + b) * size[t] + a
@@ -168,24 +200,29 @@
                 two.append(c)
     for c in heads:
         c.wait()
-    for c in sends:
-        c.wait_recv()
+    for k in range(1, NH):
+        for i in range(2):
+            kv_copy(k, i).wait_recv()
     for c in two:
         c.wait_recv()
 
+    owners = []
     for b in range(2):
         for i in range(LIST):
+            o = cite_ref[roll, list_ref[b, i]] >> 1
+            owners.append(o)
+            ox, oz, oy = o & (NX - 1), (o // NX) & 1, o // (2 * NX)
+            slots = [((oz ^ zh) * NY + oy) * NX + ox, ((oz ^ zh) * NX + ox) * NY + oy]
             rows = pl.ds(i * BLOCK, BLOCK)
             for t in range(2):
-                cat[t, b, rows] = pool[t, slot_ref[t, b * LIST + i]]
+                cat[t, b, rows] = pool[t, slots[t]]
         cat[0, b, LIST * BLOCK : KEYS] = kw[...]
         cat[1, b, LIST * BLOCK : KEYS] = vw[...]
         for t in range(2):
             cat_t[t, b] = cat[t, b].T
 
-    def compute(step, _):
-        b = step // (GROUP // 2)
-        c0 = pl.multiple_of(lax.rem(step, GROUP // 2) * 2 * HD, 2 * HD)
+    def compute(b, j):
+        c0 = pl.multiple_of(j * PAIR, PAIR)
         c1 = pl.multiple_of(c0 + HD, HD)
         rows = pl.ds(pl.multiple_of(b * BLOCK, BLOCK), BLOCK)
         cols = (pl.ds(c0, HD), pl.ds(c1, HD))
@@ -211,15 +248,60 @@
         for i, c in enumerate(cols):
             att[rows, c] = out_t[:, i * HD : (i + 1) * HD].T.astype(BF16)
             dq[rows, c] = dq_t[:, i * HD : (i + 1) * HD].T.astype(BF16)
+
+    back = ((att, att_ref, WIDE), (dq, qg_ref, WIDE), (kv_out.at[0], kg_ref, HD), (kv_out.at[1], vg_ref, HD))
+
+    def own_out(i):
+        src, dst, width = back[i]
+        there = pl.ds(pl.multiple_of(head * width, width), width)
+        return pltpu.make_async_copy(src.at[mine], dst.at[:, there], out_l.at[i])
+
+    def kv_back(k, i):
+        h = lax.rem(head + k, NH)
+        src, dst, width = back[2 + i]
+        theirs = pl.ds(pl.multiple_of(h * ROWS, ROWS), ROWS)
+        there = pl.ds(pl.multiple_of(head * width, width), width)
+        return remote(src.at[theirs], dst.at[:, there], kvo_s.at[k, i], kvo_r.at[k, i], (roll, h))
+
+    def chunk_back(k, i, j):
+        h = lax.rem(head + k, NH)
+        src, dst, width = back[i]
+        theirs = pl.ds(pl.multiple_of(h * ROWS, ROWS), ROWS)
+        return remote(
+            src.at[theirs, pl.ds(pl.multiple_of(j * PAIR, PAIR), PAIR)],
+            dst.at[:, pl.ds(pl.multiple_of(head * width + j * PAIR, PAIR), PAIR)],
+            out_s.at[k, i, j], out_r.at[k, i, j], (roll, h),
+        )
+
+    def per_chunk(j, _):
+        for k in range(1, NH):
+            for i in range(2):
+                chunk_copy(k, i, j).wait_recv()
+
+        def per_block(b, _):
+            compute(b, j)
+            return 0
+
+        lax.fori_loop(0, 2, per_block, 0)
+        for k in range(1, NH):
+            for i in range(2):
+                chunk_back(k, i, j).start()
         return 0
 
-    lax.fori_loop(0, GROUP, compute, 0)
+    lax.fori_loop(0, STEPS, per_chunk, 0)
 
     def prepare(t, p):
         def step(n, _):
             b, a = n // size[t], lax.rem(n, size[t])
-            m = p * size[0] * size[1] + n
-            total = acc[t, 0, pos_ref[t, 0, m]] + acc[t, 1, pos_ref[t, 1, m]]
+            o = at(t, a, b, zh if p == 0 else 1 - zh)
+            pos = []
+            for blk in range(2):
+                at_list = jnp.int32(NONE)
+                for i in range(LIST):
+                    same = (owners[blk * LIST + i] == o).astype(jnp.int32)
+                    at_list = at_list + same * (i - at_list)
+                pos.append(at_list)
+            total = acc[t, 0, pos[0]] + acc[t, 1, pos[1]]
             if t == 0:
                 total = total * SCALE
             gs[t, p, b, a] = total.astype(BF16)
@@ -248,24 +330,11 @@
             total = total * SCALE
         kv_out[t] = total.astype(BF16)
 
-    outs = []
-    back = (
-        (kv_out.at[0], kg_ref, HD), (kv_out.at[1], vg_ref, HD), (att, att_ref, WIDE), (dq, qg_ref, WIDE)
-    )
-    local_outs = []
-    for i, (src, dst, width) in enumerate(back):
-        there = pl.ds(pl.multiple_of(head * width, width), width)
-        c = pltpu.make_async_copy(src.at[mine], dst.at[:, there], out_l.at[i])
-        c.start()
-        local_outs.append(c)
-        for k in range(1, NH):
-            h = lax.rem(head + k, NH)
-            theirs = pl.ds(pl.multiple_of(h * ROWS, ROWS), ROWS)
-            c = remote(
-                src.at[theirs], dst.at[:, there], out_s.at[k, i], out_r.at[k, i], (roll, h)
-            )
-            c.start()
-            outs.append(c)
+    for i in range(4):
+        own_out(i).start()
+    for k in range(1, NH):
+        for i in range(2):
+            kv_back(k, i).start()
 
     back_one = [[[], []], [[], []]]
     back_z = [None, None]
@@ -316,11 +385,22 @@
         back_z[t].wait_recv()
         ref[...] = kept[t] + zr[t].astype(F32)
 
-    for c in local_outs:
-        c.wait()
-    for c in outs:
-        c.wait_recv()
-    for c in z_copy + sends + two + outs + back_z:
+    for i in range(4):
+        own_out(i).wait()
+    for k in range(1, NH):
+        for i in range(2):
+            kv_copy(k, i).wait_send()
+            kv_back(k, i).wait()
+
+    def drain(j, _):
+        for k in range(1, NH):
+            for i in range(2):
+                chunk_copy(k, i, j).wait_send()
+                chunk_back(k, i, j).wait()
+        return 0
+
+    lax.fori_loop(0, STEPS, drain, 0)
+    for c in z_copy + two + back_z:
         c.wait_send()
     for group in (one, back_two, back_one):
         for t in range(2):
@@ -329,34 +409,16 @@
                     c.wait_send()
 
 
+def copy_out(*refs):
+    n = len(refs) // 2
+    copies = [pltpu.make_async_copy(refs[i], refs[n + i], refs[-1].at[i]) for i in range(n)]
+    for c in copies:
+        c.start()
+    for c in copies:
+        c.wait()
+
+
 def local(queries, keys, values, cotangent, doc_keys, doc_values, citations, block_lists):
-    rolls = 2 * NX * NY
-    roll = lax.axis_index("roll")
-    zh = (roll // NX) % 2
-    owner = jnp.arange(rolls, dtype=jnp.int32)
-    par = jnp.sum(
-        jnp.where(citations[:, None, :] // 2 == owner[None, :, None], citations[:, None, :] % 2, 0),
-        axis=-1,
-    ).astype(F32)
-    own = lax.dynamic_slice_in_dim(citations, roll, 1, 0)[0]
-    wanted = jnp.sum(
-        jnp.where(
-            block_lists[:, :, None] == jnp.arange(own.shape[0], dtype=jnp.int32), own[None, None, :], 0
-        ),
-        axis=-1,
-    ) // 2
-    plane = (wanted // NX) % 2 ^ zh
-    wx, wy = wanted % NX, wanted // (2 * NX)
-    slots = jnp.stack([(plane * NY + wy) * NX + wx, (plane * NX + wx) * NY + wy])
-    pos = NONE + jnp.sum(
-        jnp.where(
-            slots[:, :, :, None] == owner,
-            jnp.arange(LIST, dtype=jnp.int32)[None, None, :, None] - NONE,
-            0,
-        ),
-        axis=2,
-    )
-    slots = slots.reshape(2, 2 * LIST)
     n = max(NX, NY)
     any_spec = pl.BlockSpec(memory_space=pltpu.HBM)
     vmem = pl.BlockSpec(memory_space=pltpu.VMEM)
@@ -364,13 +426,13 @@
     dma = pltpu.SemaphoreType.DMA
     blk = (BLOCK, HD)
     sd = jax.ShapeDtypeStruct
-    return pl.pallas_call(
+    results = pl.pallas_call(
         kernel,
         out_shape=(
             sd(queries.shape, BF16), sd(queries.shape, BF16), sd(keys.shape, BF16), sd(keys.shape, BF16),
             sd(doc_keys.shape, F32), sd(doc_keys.shape, F32),
         ),
-        in_specs=[any_spec] * 6 + [smem] * 3,
+        in_specs=[any_spec] * 6 + [vmem, smem, smem],
         out_specs=(any_spec,) * 4 + (vmem,) * 2,
         scratch_shapes=[
             pltpu.VMEM((QTOK, WIDE), BF16),
@@ -392,16 +454,29 @@
             pltpu.VMEM((2, 2, n, 2 * BLOCK, HD), BF16),
             pltpu.VMEM((2, 2 * BLOCK, HD), BF16),
             pltpu.VMEM((2, 2 * BLOCK, HD), BF16),
-            dma((4,)), dma((2,)), dma((NH, 4)), dma((NH, 4)), dma((2,)), dma((2,)),
+            pltpu.VMEM((2 * NX * NY, HD), F32),
+            pltpu.SMEM((2 * NX * NY, HD), F32),
+            dma((1,)),
+            dma((4,)), dma((2,)), dma((NH, 2)), dma((NH, 2)), dma((NH, 2, STEPS)), dma((NH, 2, STEPS)),
+            dma((2,)), dma((2,)),
             dma((2, 2, n)), dma((2, 2, n)), dma((2, 2, n)), dma((2, 2, n)),
-            dma((NH, 4)), dma((NH, 4)), dma((4,)),
+            dma((NH, 2)), dma((NH, 2)), dma((NH, 2, STEPS)), dma((NH, 2, STEPS)), dma((4,)),
             dma((2, 2, n)), dma((2, 2, n)), dma((2, 2, n)), dma((2, 2, n)), dma((2,)), dma((2,)),
         ],
         compiler_params=pltpu.CompilerParams(
-            collective_id=0, has_side_effects=True, vmem_limit_bytes=48 * 2**20
+            collective_id=0, has_side_effects=True, vmem_limit_bytes=60 * 2**20
         ),
         name="attention",
-    )(queries, cotangent, keys, values, doc_keys, doc_values, par, slots, pos)
+    )(queries, cotangent, keys, values, doc_keys, doc_values, citations, citations, block_lists)
+    return pl.pallas_call(
+        copy_out,
+        out_shape=tuple(sd(r.shape, r.dtype) for r in results),
+        in_specs=[any_spec] * 6,
+        out_specs=(any_spec,) * 6,
+        scratch_shapes=[dma((6,))],
+        compiler_params=pltpu.CompilerParams(vmem_limit_bytes=60 * 2**20),
+        name="copy_out",
+    )(*results)
 
 
 def solution(mesh):

time: 90.6 us -> 132 us (1.46)
  Pallas kernels: 81.1 us -> 130 us
  local copies, waits for them, and re-layouts: 7.79 us -> 1.38 us
    pallas_call x0 -> x1, Pallas kernels: none -> 44.8 us  [local(): pl.pallas_call(copy_out, out_shape=tuple((sd(r.shape, r.dtype) for r in r...]
    unnamed x22 -> x1, local copies, waits for them, and re-layouts: 7.38 us -> 1.38 us
    pallas_call x1, Pallas kernels: 81.1 us -> 85.2 us  [local(): pl.pallas_call(kernel, out_shape=(sd(queries.shape, BF16), sd(queries.sha...]
where the time goes in v2:
time: 132 us
  Pallas kernels  130 us (98%)
  local copies, waits for them, and re-layouts  1.38 us (1%)
    pallas_call x1, Pallas kernels, local(): pl.pallas_call(kernel, out_shape=(sd(queries.shape, BF16), sd(queries.sha...  85.2 us
    pallas_call x1, Pallas kernels, local(): pl.pallas_call(copy_out, out_shape=tuple((sd(r.shape, r.dtype) for r in r...  44.8 us

profile of v2, /device:TPU:33, one launch (start us, length us, event | category | flops | bytes accessed | tf_op | source)
XLA Modules:
  0.0 132.0 jit_solution(14569983001971100558)
XLA Ops:
  0.6 1.4 %copy.14.cite_v_ref.cite_ref = s32[32,16]{1,0:T(8,128)} copy(s32[32,16]{0,1:T(8,128)} %param.14) | data formatting | bytes 4096 | tf_op args[6]
  2.0 85.2 %attention.1 = (bf16[32,8192]{1,0:T(8,128)(2,1)}, bf16[32,8192]{1,0:T(8,128)(2,1)}, bf16[32,1024]{1,0:T(8,128)(2,1)}, bf16[32,1024]{1,0:T(8,128)(2,1)}, f32[256,128]{1,0:T(8,128)}, /*index=5*/f32[256,128]{1,0:T(8,128)}) custom-call(bf16[32,8192]{1,0:T(8,128)(2,1)} %q_ref.1, bf16[32,8192]{1,0:T(8,128)(2,1)} %g_ref.1, bf16[32,1024]{1,0:T(8,128)(2,1)} %k_ref.1, ...), custom_call_target="tpu_custom_call" | custom-call | tf_op jit(solution)/shard_map/attention/pallas_call | solution.py:429
  87.2 44.8 %copy_out.1 = (bf16[32,8192]{1,0:T(8,128)(2,1)}, bf16[32,8192]{1,0:T(8,128)(2,1)}, bf16[32,1024]{1,0:T(8,128)(2,1)}, bf16[32,1024]{1,0:T(8,128)(2,1)}, f32[256,128]{1,0:T(8,128)}, /*index=5*/f32[256,128]{1,0:T(8,128)}) custom-call(bf16[32,8192]{1,0:T(8,128)(2,1)} %get-tuple-element.12.refs_0_, bf16[32,8192]{1,0:T(8,128)(2,1)} %get-tuple-element.13.refs_1_, ...), custom_call_target="tpu_custom_call" | custom-call | tf_op jit(solution)/shard_map/copy_out/pallas_call | solution.py:471

commit v3 on v2

--- a/solution.py
+++ b/solution.py
@@ -22,6 +22,8 @@
 NONE = KEYS // BLOCK
 PAIR = 2 * HD
 STEPS = GROUP // 2
+EARLY = 1
+MIDDLE = 4
 MESH = pl.DeviceIdType.MESH
 SCALE = 1.0 / math.sqrt(HD)
 LOG2E = math.log2(math.e)
@@ -71,25 +73,26 @@
             src_ref=src, dst_ref=dst, send_sem=ss, recv_sem=rs, device_id=dev, device_id_type=MESH
         )
 
-    acc[...] = jnp.zeros_like(acc)
-
-    cites = cite_v_ref[...]
-    rolls = 2 * NX * NY
-    owner_at = lax.broadcasted_iota(jnp.int32, (rolls, HD), 1)
-    odd = jnp.zeros((rolls, HD), jnp.int32)
-    for c in range(cites.shape[1]):
-        cite = cites[:, c : c + 1]
-        odd = odd + jnp.where((cite >> 1) == owner_at, cite & 1, 0)
-
     barrier = pltpu.get_barrier_semaphore()
     partners = [z_dev]
     partners += [first(t, d) for t in range(2) for d in range(1, size[t])]
     partners += [(roll, lax.rem(head + k, NH)) for k in range(1, NH)]
     for dev in partners:
         pl.semaphore_signal(barrier, inc=1, device_id=dev, device_id_type=MESH)
+
+    acc[...] = jnp.zeros_like(acc)
+
+    cites = cite_v_ref[...]
+    rolls = 2 * NX * NY
+    owner_at = lax.broadcasted_iota(jnp.int32, (rolls, rolls), 0)
+    odd = jnp.zeros((rolls, rolls), jnp.int32)
+    for c in range(cites.shape[0]):
+        cite = cites[c : c + 1]
+        odd = odd + jnp.where((cite >> 1) == owner_at, cite & 1, 0)
+
     pl.semaphore_wait(barrier, len(partners))
 
-    par_v[...] = odd.astype(F32)
+    par_v[:, 0:rolls] = odd.astype(F32)
     par_copy = pltpu.make_async_copy(par_v, par_ref, par_sem.at[0])
 
     z_copy = []
@@ -161,7 +164,7 @@
             target = second(t, d)[0]
 
             def step(a, _):
-                pr = par_ref[target, at(t, a, place[1 - t], o_z)]
+                pr = par_ref[at(t, a, place[1 - t], o_z), target]
                 low = ag[t, p, a, 0:BLOCK].astype(F32)
                 high = ag[t, p, a, BLOCK : 2 * BLOCK].astype(F32)
                 chosen = (low * (1.0 - pr) + high * pr).astype(BF16)
@@ -209,7 +212,7 @@
     owners = []
     for b in range(2):
         for i in range(LIST):
-            o = cite_ref[roll, list_ref[b, i]] >> 1
+            o = cite_ref[list_ref[b, i], roll] >> 1
             owners.append(o)
             ox, oz, oy = o & (NX - 1), (o // NX) & 1, o // (2 * NX)
             slots = [((oz ^ zh) * NY + oy) * NX + ox, ((oz ^ zh) * NX + ox) * NY + oy]
@@ -273,6 +276,12 @@
             out_s.at[k, i, j], out_r.at[k, i, j], (roll, h),
         )
 
+    def send_back(j, _):
+        for k in range(1, NH):
+            for i in range(2):
+                chunk_back(k, i, j).start()
+        return 0
+
     def per_chunk(j, _):
         for k in range(1, NH):
             for i in range(2):
@@ -283,16 +292,16 @@
             return 0
 
         lax.fori_loop(0, 2, per_block, 0)
-        for k in range(1, NH):
-            for i in range(2):
-                chunk_back(k, i, j).start()
+        @pl.when(j < EARLY)
+        def _():
+            send_back(j, 0)
+
         return 0
 
     lax.fori_loop(0, STEPS, per_chunk, 0)
 
-    def prepare(t, p):
-        def step(n, _):
-            b, a = n // size[t], lax.rem(n, size[t])
+    def prepare(t, p, b):
+        def step(a, _):
             o = at(t, a, b, zh if p == 0 else 1 - zh)
             pos = []
             for blk in range(2):
@@ -307,22 +316,26 @@
             gs[t, p, b, a] = total.astype(BF16)
             return 0
 
-        lax.fori_loop(0, size[0] * size[1], step, 0)
-        b = place[1 - t]
-        gr[t, p, b] = gs[t, p, b]
+        lax.fori_loop(0, size[t], step, 0)
 
     back_two = [[[], []], [[], []]]
     for p in (1, 0):
-        for t in range(2):
-            prepare(t, p)
-            for d in range(1, size[1 - t]):
+        for d in range(1, NX):
+            for t in range(2):
                 b = lax.rem(place[1 - t] + d, size[1 - t])
+                prepare(t, p, b)
                 c = remote(
                     gs.at[t, p, b], gr.at[t, p, place[1 - t]],
                     two_bs.at[t, p, d], two_br.at[t, p, d], second(t, d),
                 )
                 c.start()
                 back_two[t][p].append(c)
+    lax.fori_loop(EARLY, MIDDLE, send_back, 0)
+    for p in (1, 0):
+        for t in range(2):
+            b = place[1 - t]
+            prepare(t, p, b)
+            gr[t, p, b] = gs[t, p, b]
 
     for t in range(2):
         total = (acc[t, 0, LIST:NONE] + acc[t, 1, LIST:NONE]).reshape(QTOK, HD)
@@ -337,27 +350,30 @@
             kv_back(k, i).start()
 
     back_one = [[[], []], [[], []]]
-    back_z = [None, None]
-    kept = [None, None]
+    back_z = []
+
+    def merge_rolls(t, p):
+        o_z = zh if p == 0 else 1 - zh
+
+        def merge(a, _):
+            o = at(t, a, place[1 - t], o_z)
+            low = high = jnp.zeros((BLOCK, HD), F32)
+            for b in range(size[1 - t]):
+                pr = par_ref[o, at(t, place[t], b, zh)]
+                m = gr[t, p, b, a].astype(F32)
+                low = low + m * (1.0 - pr)
+                high = high + m * pr
+            s1[t, p, a, 0:BLOCK] = low.astype(BF16)
+            s1[t, p, a, BLOCK : 2 * BLOCK] = high.astype(BF16)
+            return 0
+
+        lax.fori_loop(0, size[t], merge, 0)
+
     for p in (1, 0):
-        o_z = zh if p == 0 else 1 - zh
         for t in range(2):
             for c in back_two[t][p]:
                 c.wait_recv()
-
-            def merge(a, _):
-                o = at(t, a, place[1 - t], o_z)
-                low = high = jnp.zeros((BLOCK, HD), F32)
-                for b in range(size[1 - t]):
-                    pr = par_ref[at(t, place[t], b, zh), o]
-                    m = gr[t, p, b, a].astype(F32)
-                    low = low + m * (1.0 - pr)
-                    high = high + m * pr
-                s1[t, p, a, 0:BLOCK] = low.astype(BF16)
-                s1[t, p, a, BLOCK : 2 * BLOCK] = high.astype(BF16)
-                return 0
-
-            lax.fori_loop(0, size[t], merge, 0)
+            merge_rolls(t, p)
             for d in range(1, size[t]):
                 a = lax.rem(place[t] + d, size[t])
                 c = remote(
@@ -367,7 +383,8 @@
                 c.start()
                 back_one[t][p].append(c)
             r1[t, p, place[t]] = s1[t, p, place[t]]
-    for p in (1, 0):
+        if p == 1:
+            lax.fori_loop(MIDDLE, STEPS, send_back, 0)
         for t in range(2):
             for c in back_one[t][p]:
                 c.wait_recv()
@@ -378,12 +395,10 @@
                 zs[t] = total.astype(BF16)
                 c = remote(zs.at[t], zr.at[t], zb_s.at[t], zb_r.at[t], z_dev)
                 c.start()
-                back_z[t] = c
+                back_z.append(c)
             else:
-                kept[t] = total
-    for t, ref in enumerate((dkg_ref, dvg_ref)):
-        back_z[t].wait_recv()
-        ref[...] = kept[t] + zr[t].astype(F32)
+                back_z[t].wait_recv()
+                (dkg_ref, dvg_ref)[t][...] = total + zr[t].astype(F32)
 
     for i in range(4):
         own_out(i).wait()
@@ -410,11 +425,16 @@
 
 
 def copy_out(*refs):
-    n = len(refs) // 2
-    copies = [pltpu.make_async_copy(refs[i], refs[n + i], refs[-1].at[i]) for i in range(n)]
-    for c in copies:
+    n = (len(refs) - 1) // 3
+    src, dst, held, sem = refs[:n], refs[n : 2 * n], refs[2 * n : 3 * n], refs[-1]
+    into = [pltpu.make_async_copy(src[i], held[i], sem.at[0, i]) for i in range(n)]
+    back = [pltpu.make_async_copy(held[i], dst[i], sem.at[1, i]) for i in range(n)]
+    for c in into:
         c.start()
-    for c in copies:
+    for i in range(n):
+        into[i].wait()
+        back[i].start()
+    for c in back:
         c.wait()
 
 
@@ -467,13 +487,13 @@
             collective_id=0, has_side_effects=True, vmem_limit_bytes=60 * 2**20
         ),
         name="attention",
-    )(queries, cotangent, keys, values, doc_keys, doc_values, citations, citations, block_lists)
+    )(queries, cotangent, keys, values, doc_keys, doc_values, citations.T, citations.T, block_lists)
     return pl.pallas_call(
         copy_out,
         out_shape=tuple(sd(r.shape, r.dtype) for r in results),
         in_specs=[any_spec] * 6,
         out_specs=(any_spec,) * 6,
-        scratch_shapes=[dma((6,))],
+        scratch_shapes=[pltpu.VMEM(r.shape, r.dtype) for r in results] + [dma((2, 6))],
         compiler_params=pltpu.CompilerParams(vmem_limit_bytes=60 * 2**20),
         name="copy_out",
     )(*results)

time: 132 us -> 82.6 us (0.63)
  Pallas kernels: 130 us -> 81.3 us
  local copies, waits for them, and re-layouts: 1.38 us -> 0 us
    pallas_call x1, Pallas kernels: 44.8 us -> 2.23 us  [local(): pl.pallas_call(copy_out, out_shape=tuple((sd(r.shape, r.dtype) for r in r...]
    pallas_call x1, Pallas kernels: 85.2 us -> 79.1 us  [local(): pl.pallas_call(kernel, out_shape=(sd(queries.shape, BF16), sd(queries.sha...]
    unnamed x1 -> x0, local copies, waits for them, and re-layouts: 1.38 us -> none
where the time goes in v3:
time: 82.6 us; the launch traced here: 81.9 us
  Pallas kernels  81.3 us (98%)
    pallas_call x1, Pallas kernels, local(): pl.pallas_call(kernel, out_shape=(sd(queries.shape, BF16), sd(queries.sha...  79.1 us
    pallas_call x1, Pallas kernels, local(): pl.pallas_call(copy_out, out_shape=tuple((sd(r.shape, r.dtype) for r in r...  2.23 us

profile of v3, /device:TPU:33, one launch (start us, length us, event | category | flops | bytes accessed | tf_op | source)
XLA Modules:
  0.0 81.9 jit_solution(15697572241601126978)
XLA Ops:
  0.6 79.1 %attention.1 = (bf16[32,8192]{1,0:T(8,128)(2,1)}, bf16[32,8192]{1,0:T(8,128)(2,1)}, bf16[32,1024]{1,0:T(8,128)(2,1)}, bf16[32,1024]{1,0:T(8,128)(2,1)}, f32[256,128]{1,0:T(8,128)}, /*index=5*/f32[256,128]{1,0:T(8,128)}) custom-call(bf16[32,8192]{1,0:T(8,128)(2,1)} %q_ref.1, bf16[32,8192]{1,0:T(8,128)(2,1)} %g_ref.1, bf16[32,1024]{1,0:T(8,128)(2,1)} %k_ref.1, ...), custom_call_target="tpu_custom_call" | custom-call | tf_op jit(solution)/shard_map/attention/pallas_call | solution.py:449
  79.7 2.2 %copy_out.1 = (bf16[32,8192]{1,0:T(8,128)(2,1)}, bf16[32,8192]{1,0:T(8,128)(2,1)}, bf16[32,1024]{1,0:T(8,128)(2,1)}, bf16[32,1024]{1,0:T(8,128)(2,1)}, f32[256,128]{1,0:T(8,128)}, /*index=5*/f32[256,128]{1,0:T(8,128)}) custom-call(bf16[32,8192]{1,0:T(8,128)(2,1)} %get-tuple-element.12.refs_0_, bf16[32,8192]{1,0:T(8,128)(2,1)} %get-tuple-element.13.refs_1_, ...), custom_call_target="tpu_custom_call" | custom-call | tf_op jit(solution)/shard_map/copy_out/pallas_call | solution.py:491

commit v4 on v3

--- a/solution.py
+++ b/solution.py
@@ -22,8 +22,10 @@
 NONE = KEYS // BLOCK
 PAIR = 2 * HD
 STEPS = GROUP // 2
-EARLY = 1
-MIDDLE = 4
+CUTS = (2, 3, 4, 4)
+LAG = 1
+VMEM_MIB = 56
+ORDER_OUT = (4, 3, 5, 2, 6, 1, 7)
 MESH = pl.DeviceIdType.MESH
 SCALE = 1.0 / math.sqrt(HD)
 LOG2E = math.log2(math.e)
@@ -43,7 +45,7 @@
     q_ref, g_ref, k_ref, v_ref, dk_ref, dv_ref, cite_v_ref, cite_ref, list_ref,
     att_ref, qg_ref, kg_ref, vg_ref, dkg_ref, dvg_ref,
     qw, gw, kw, vw, ag, sel, pool, cat, cat_t, acc, att, dq, kv_out, gs, gr, s1, r1, zs, zr,
-    par_v, par_ref, par_sem, own_q, own_doc, kv_s, kv_r, head_s, head_r, z_s, z_r, one_s, one_r, two_s, two_r,
+    par_v, par_ref, pos_ref, par_sem, own_q, own_doc, kv_s, kv_r, head_s, head_r, z_s, z_r, one_s, one_r, two_s, two_r,
     kvo_s, kvo_r, out_s, out_r, out_l, two_bs, two_br, one_bs, one_br, zb_s, zb_r,
 ):
     roll = lax.axis_index("roll")
@@ -73,6 +75,9 @@
             src_ref=src, dst_ref=dst, send_sem=ss, recv_sem=rs, device_id=dev, device_id_type=MESH
         )
 
+    def landed(ref, sem):
+        pltpu.make_async_copy(ref, ref, sem).wait()
+
     barrier = pltpu.get_barrier_semaphore()
     partners = [z_dev]
     partners += [first(t, d) for t in range(2) for d in range(1, size[t])]
@@ -80,40 +85,24 @@
     for dev in partners:
         pl.semaphore_signal(barrier, inc=1, device_id=dev, device_id_type=MESH)
 
-    acc[...] = jnp.zeros_like(acc)
-
-    cites = cite_v_ref[...]
-    rolls = 2 * NX * NY
-    owner_at = lax.broadcasted_iota(jnp.int32, (rolls, rolls), 0)
-    odd = jnp.zeros((rolls, rolls), jnp.int32)
-    for c in range(cites.shape[0]):
-        cite = cites[c : c + 1]
-        odd = odd + jnp.where((cite >> 1) == owner_at, cite & 1, 0)
-
     pl.semaphore_wait(barrier, len(partners))
-
-    par_v[:, 0:rolls] = odd.astype(F32)
-    par_copy = pltpu.make_async_copy(par_v, par_ref, par_sem.at[0])
 
     z_copy = []
     for t in range(2):
         c = remote(docs[t], ag.at[t, 1, place[t]], z_s.at[t], z_r.at[t], z_dev)
         c.start()
         z_copy.append(c)
-    one = [[[], []], [[], []]]
     for t in range(2):
         for d in range(1, size[t]):
             c = remote(
-                docs[t], ag.at[t, 0, place[t]], one_s.at[t, 0, d], one_r.at[t, 0, d], first(t, d)
+                docs[t], ag.at[t, 0, place[t]], one_s.at[t, 0], one_r.at[t, 0], first(t, d)
             )
             c.start()
-            one[t][0].append(c)
     own_docs = []
     for t in range(2):
         c = pltpu.make_async_copy(docs[t], ag.at[t, 0, place[t]], own_doc.at[t])
         c.start()
         own_docs.append(c)
-    par_copy.start()
     heads = []
     mine = pl.ds(pl.multiple_of(head * ROWS, ROWS), ROWS)
     moved = ((k_ref, kw, HD), (v_ref, vw, HD), (q_ref, qw, WIDE), (g_ref, gw, WIDE))
@@ -129,7 +118,7 @@
         src, dst, width = moved[i]
         return remote(
             src.at[:, pl.ds(pl.multiple_of(h * width, width), width)],
-            dst.at[mine], kv_s.at[k, i], kv_r.at[k, i], (roll, h),
+            dst.at[mine], kv_s.at[i], kv_r.at[i], (roll, h),
         )
 
     def chunk_copy(k, i, j):
@@ -138,7 +127,7 @@
         return remote(
             src.at[:, pl.ds(pl.multiple_of(h * width + j * PAIR, PAIR), PAIR)],
             dst.at[mine, pl.ds(pl.multiple_of(j * PAIR, PAIR), PAIR)],
-            head_s.at[k, i, j], head_r.at[k, i, j], (roll, h),
+            head_s.at[i], head_r.at[i, j], (roll, h),
         )
 
     for k in range(1, NH):
@@ -153,7 +142,32 @@
 
     lax.fori_loop(0, STEPS, send_chunks, 0)
 
+    cites = cite_v_ref[...]
+    rolls = 2 * NX * NY
+    owner_at = lax.broadcasted_iota(jnp.int32, (rolls, rolls), 0)
+    odd = jnp.zeros((rolls, rolls), jnp.int32)
+    for c in range(cites.shape[0]):
+        cite = cites[c : c + 1]
+        odd = odd + jnp.where((cite >> 1) == owner_at, cite & 1, 0)
+
+    par_v[:, 0:rolls] = odd.astype(F32)
+    par_copy = pltpu.make_async_copy(par_v, par_ref, par_sem.at[0])
+    par_copy.start()
+    acc[...] = jnp.zeros_like(acc)
     par_copy.wait()
+
+    owners = [[cite_ref[list_ref[b, i], roll] >> 1 for i in range(LIST)] for b in range(2)]
+
+    def find(o, _):
+        for b in range(2):
+            found = jnp.int32(NONE)
+            for i in range(LIST):
+                same = (owners[b][i] == o).astype(jnp.int32)
+                found = found + same * (i - found)
+            pos_ref[b, o] = found
+        return 0
+
+    lax.fori_loop(0, rolls, find, 0)
 
     def slot(t, p, b, a):
         return (p * size[1 - t] + b) * size[t] + a
@@ -176,7 +190,6 @@
 
             lax.fori_loop(0, size[t], step, 0)
 
-    two = []
     for p in range(2):
         if p == 1:
             for t in range(2):
@@ -184,36 +197,32 @@
                 for d in range(1, size[t]):
                     c = remote(
                         ag.at[t, 1, place[t]], ag.at[t, 1, place[t]],
-                        one_s.at[t, 1, d], one_r.at[t, 1, d], first(t, d),
+                        one_s.at[t, 1], one_r.at[t, 1], first(t, d),
                     )
                     c.start()
-                    one[t][1].append(c)
         for t in range(2):
             if p == 0:
                 own_docs[t].wait()
-            for c in one[t][p]:
-                c.wait_recv()
+            landed(ag.at[t, p, 0 : size[t] - 1], one_r.at[t, p])
             pick(t, p)
             for d in range(1, size[1 - t]):
                 c = remote(
                     sel.at[t, p, d - 1], pool.at[t, pl.ds(slot(t, p, place[1 - t], 0), size[t])],
-                    two_s.at[t, p, d], two_r.at[t, p, d], second(t, d),
+                    two_s.at[t, p], two_r.at[t, p], second(t, d),
                 )
                 c.start()
-                two.append(c)
     for c in heads:
         c.wait()
-    for k in range(1, NH):
-        for i in range(2):
-            kv_copy(k, i).wait_recv()
-    for c in two:
-        c.wait_recv()
-
-    owners = []
+    others = QTOK - ROWS
+    for i, ref in enumerate((kw, vw)):
+        landed(ref.at[0:others], kv_r.at[i])
+    for t in range(2):
+        for p in range(2):
+            landed(pool.at[t, 0 : (size[1 - t] - 1) * size[t]], two_r.at[t, p])
+
     for b in range(2):
         for i in range(LIST):
-            o = cite_ref[list_ref[b, i], roll] >> 1
-            owners.append(o)
+            o = owners[b][i]
             ox, oz, oy = o & (NX - 1), (o // NX) & 1, o // (2 * NX)
             slots = [((oz ^ zh) * NY + oy) * NX + ox, ((oz ^ zh) * NX + ox) * NY + oy]
             rows = pl.ds(i * BLOCK, BLOCK)
@@ -264,7 +273,7 @@
         src, dst, width = back[2 + i]
         theirs = pl.ds(pl.multiple_of(h * ROWS, ROWS), ROWS)
         there = pl.ds(pl.multiple_of(head * width, width), width)
-        return remote(src.at[theirs], dst.at[:, there], kvo_s.at[k, i], kvo_r.at[k, i], (roll, h))
+        return remote(src.at[theirs], dst.at[:, there], kvo_s.at[i], kvo_r.at[i], (roll, h))
 
     def chunk_back(k, i, j):
         h = lax.rem(head + k, NH)
@@ -273,28 +282,27 @@
         return remote(
             src.at[theirs, pl.ds(pl.multiple_of(j * PAIR, PAIR), PAIR)],
             dst.at[:, pl.ds(pl.multiple_of(head * width + j * PAIR, PAIR), PAIR)],
-            out_s.at[k, i, j], out_r.at[k, i, j], (roll, h),
+            out_s.at[i], out_r.at[i], (roll, h),
         )
 
     def send_back(j, _):
-        for k in range(1, NH):
+        for k in ORDER_OUT:
             for i in range(2):
                 chunk_back(k, i, j).start()
         return 0
 
     def per_chunk(j, _):
-        for k in range(1, NH):
-            for i in range(2):
-                chunk_copy(k, i, j).wait_recv()
+        for i, ref in enumerate((qw, gw)):
+            landed(ref.at[0:others, pl.ds(pl.multiple_of(j * PAIR, PAIR), PAIR)], head_r.at[i, j])
 
         def per_block(b, _):
             compute(b, j)
             return 0
 
         lax.fori_loop(0, 2, per_block, 0)
-        @pl.when(j < EARLY)
+        @pl.when((j >= LAG) & (j < CUTS[0] + LAG))
         def _():
-            send_back(j, 0)
+            send_back(j - LAG, 0)
 
         return 0
 
@@ -303,22 +311,14 @@
     def prepare(t, p, b):
         def step(a, _):
             o = at(t, a, b, zh if p == 0 else 1 - zh)
-            pos = []
-            for blk in range(2):
-                at_list = jnp.int32(NONE)
-                for i in range(LIST):
-                    same = (owners[blk * LIST + i] == o).astype(jnp.int32)
-                    at_list = at_list + same * (i - at_list)
-                pos.append(at_list)
-            total = acc[t, 0, pos[0]] + acc[t, 1, pos[1]]
+            total = acc[t, 0, pos_ref[0, o]] + acc[t, 1, pos_ref[1, o]]
             if t == 0:
                 total = total * SCALE
             gs[t, p, b, a] = total.astype(BF16)
-            return 0
-
-        lax.fori_loop(0, size[t], step, 0)
-
-    back_two = [[[], []], [[], []]]
+
+        for a in range(size[t]):
+            step(a, 0)
+
     for p in (1, 0):
         for d in range(1, NX):
             for t in range(2):
@@ -326,11 +326,10 @@
                 prepare(t, p, b)
                 c = remote(
                     gs.at[t, p, b], gr.at[t, p, place[1 - t]],
-                    two_bs.at[t, p, d], two_br.at[t, p, d], second(t, d),
+                    two_bs.at[t, p], two_br.at[t, p], second(t, d),
                 )
                 c.start()
-                back_two[t][p].append(c)
-    lax.fori_loop(EARLY, MIDDLE, send_back, 0)
+    lax.fori_loop(CUTS[0], CUTS[1], send_back, 0)
     for p in (1, 0):
         for t in range(2):
             b = place[1 - t]
@@ -349,7 +348,6 @@
         for i in range(2):
             kv_back(k, i).start()
 
-    back_one = [[[], []], [[], []]]
     back_z = []
 
     def merge_rolls(t, p):
@@ -370,24 +368,36 @@
         lax.fori_loop(0, size[t], merge, 0)
 
     for p in (1, 0):
+        if p == 0:
+            lax.fori_loop(CUTS[2], CUTS[3], send_back, 0)
+            for c in z_copy:
+                c.wait_send()
+            for i, ref in enumerate((kw, vw)):
+                landed(ref.at[0:others], kv_s.at[i])
+            for i, ref in enumerate((qw, gw)):
+                landed(ref.at[0:others], head_s.at[i])
+            for t in range(2):
+                for q in range(2):
+                    landed(ag.at[t, q, 0 : size[t] - 1], one_s.at[t, q])
+                    landed(sel.at[t, q], two_s.at[t, q])
+                landed(gs.at[t, 1, 0 : size[1 - t] - 1], two_bs.at[t, 1])
+            for i in range(4):
+                own_out(i).wait()
         for t in range(2):
-            for c in back_two[t][p]:
-                c.wait_recv()
+            landed(gr.at[t, p, 0 : size[1 - t] - 1], two_br.at[t, p])
             merge_rolls(t, p)
             for d in range(1, size[t]):
                 a = lax.rem(place[t] + d, size[t])
                 c = remote(
                     s1.at[t, p, a], r1.at[t, p, place[t]],
-                    one_bs.at[t, p, d], one_br.at[t, p, d], first(t, d),
+                    one_bs.at[t, p], one_br.at[t, p], first(t, d),
                 )
                 c.start()
-                back_one[t][p].append(c)
             r1[t, p, place[t]] = s1[t, p, place[t]]
         if p == 1:
-            lax.fori_loop(MIDDLE, STEPS, send_back, 0)
+            lax.fori_loop(CUTS[1], CUTS[2], send_back, 0)
         for t in range(2):
-            for c in back_one[t][p]:
-                c.wait_recv()
+            landed(r1.at[t, p, 0 : size[t] - 1], one_br.at[t, p])
             total = r1[t, p, 0].astype(F32)
             for a in range(1, size[t]):
                 total = total + r1[t, p, a].astype(F32)
@@ -397,44 +407,30 @@
                 c.start()
                 back_z.append(c)
             else:
+                if t == 0:
+                    lax.fori_loop(CUTS[3], STEPS, send_back, 0)
+                    for i in range(2):
+                        for u in range(2):
+                            landed(r1.at[u, i, 0 : size[u] - 1], one_bs.at[u, i])
+                        landed(gs.at[i, 0, 0 : size[1 - i] - 1], two_bs.at[i, 0])
+                        landed(kg_ref.at[:, 0 : HD * (NH - 1)], kvo_r.at[i])
+                        landed(kv_out.at[i, 0:others], kvo_s.at[i])
+                        landed(att.at[0:others], out_s.at[i])
                 back_z[t].wait_recv()
                 (dkg_ref, dvg_ref)[t][...] = total + zr[t].astype(F32)
 
-    for i in range(4):
-        own_out(i).wait()
-    for k in range(1, NH):
-        for i in range(2):
-            kv_copy(k, i).wait_send()
-            kv_back(k, i).wait()
-
-    def drain(j, _):
-        for k in range(1, NH):
-            for i in range(2):
-                chunk_copy(k, i, j).wait_send()
-                chunk_back(k, i, j).wait()
-        return 0
-
-    lax.fori_loop(0, STEPS, drain, 0)
-    for c in z_copy + two + back_z:
+    for i in range(2):
+        landed(att_ref.at[:, 0 : WIDE * (NH - 1)], out_r.at[i])
+    for c in back_z:
         c.wait_send()
-    for group in (one, back_two, back_one):
-        for t in range(2):
-            for p in range(2):
-                for c in group[t][p]:
-                    c.wait_send()
 
 
 def copy_out(*refs):
-    n = (len(refs) - 1) // 3
-    src, dst, held, sem = refs[:n], refs[n : 2 * n], refs[2 * n : 3 * n], refs[-1]
-    into = [pltpu.make_async_copy(src[i], held[i], sem.at[0, i]) for i in range(n)]
-    back = [pltpu.make_async_copy(held[i], dst[i], sem.at[1, i]) for i in range(n)]
-    for c in into:
+    n = len(refs) // 2
+    copies = [pltpu.make_async_copy(refs[i], refs[n + i], refs[-1].at[i]) for i in range(n)]
+    for c in copies:
         c.start()
-    for i in range(n):
-        into[i].wait()
-        back[i].start()
-    for c in back:
+    for c in copies:
         c.wait()
 
 
@@ -449,11 +445,12 @@
     results = pl.pallas_call(
         kernel,
         out_shape=(
-            sd(queries.shape, BF16), sd(queries.shape, BF16), sd(keys.shape, BF16), sd(keys.shape, BF16),
-            sd(doc_keys.shape, F32), sd(doc_keys.shape, F32),
+            pltpu.VMEM(queries.shape, BF16), pltpu.VMEM(queries.shape, BF16),
+            pltpu.VMEM(keys.shape, BF16), pltpu.VMEM(keys.shape, BF16),
+            pltpu.VMEM(doc_keys.shape, F32), pltpu.VMEM(doc_keys.shape, F32),
         ),
         in_specs=[any_spec] * 6 + [vmem, smem, smem],
-        out_specs=(any_spec,) * 4 + (vmem,) * 2,
+        out_specs=(vmem,) * 6,
         scratch_shapes=[
             pltpu.VMEM((QTOK, WIDE), BF16),
             pltpu.VMEM((QTOK, WIDE), BF16),
@@ -476,27 +473,28 @@
             pltpu.VMEM((2, 2 * BLOCK, HD), BF16),
             pltpu.VMEM((2 * NX * NY, HD), F32),
             pltpu.SMEM((2 * NX * NY, HD), F32),
+            pltpu.SMEM((2, 2 * NX * NY), jnp.int32),
             dma((1,)),
-            dma((4,)), dma((2,)), dma((NH, 2)), dma((NH, 2)), dma((NH, 2, STEPS)), dma((NH, 2, STEPS)),
+            dma((4,)), dma((2,)), dma((2,)), dma((2,)), dma((2,)), dma((2, STEPS)),
             dma((2,)), dma((2,)),
-            dma((2, 2, n)), dma((2, 2, n)), dma((2, 2, n)), dma((2, 2, n)),
-            dma((NH, 2)), dma((NH, 2)), dma((NH, 2, STEPS)), dma((NH, 2, STEPS)), dma((4,)),
-            dma((2, 2, n)), dma((2, 2, n)), dma((2, 2, n)), dma((2, 2, n)), dma((2,)), dma((2,)),
+            dma((2, 2)), dma((2, 2)), dma((2, 2)), dma((2, 2)),
+            dma((2,)), dma((2,)), dma((2,)), dma((2,)), dma((4,)),
+            dma((2, 2)), dma((2, 2)), dma((2, 2)), dma((2, 2)), dma((2,)), dma((2,)),
         ],
         compiler_params=pltpu.CompilerParams(
-            collective_id=0, has_side_effects=True, vmem_limit_bytes=60 * 2**20
+            collective_id=0, has_side_effects=True, vmem_limit_bytes=VMEM_MIB * 2**20
         ),
         name="attention",
-    )(queries, cotangent, keys, values, doc_keys, doc_values, citations.T, citations.T, block_lists)
+    )(*[pltpu.with_memory_space_constraint(r, pltpu.HBM) for r in (queries, cotangent, keys, values, doc_keys, doc_values)], citations.T, citations.T, block_lists)
     return pl.pallas_call(
         copy_out,
         out_shape=tuple(sd(r.shape, r.dtype) for r in results),
-        in_specs=[any_spec] * 6,
+        in_specs=[vmem] * 6,
         out_specs=(any_spec,) * 6,
-        scratch_shapes=[pltpu.VMEM(r.shape, r.dtype) for r in results] + [dma((2, 6))],
-        compiler_params=pltpu.CompilerParams(vmem_limit_bytes=60 * 2**20),
+        scratch_shapes=[dma((6,))],
+        compiler_params=pltpu.CompilerParams(vmem_limit_bytes=VMEM_MIB * 2**20),
         name="copy_out",
-    )(*results)
+    )(*[pltpu.with_memory_space_constraint(r, pltpu.VMEM) for r in results])
 
 
 def solution(mesh):

time: 82.6 us -> 74 us (0.90)
  Pallas kernels: 81.3 us -> 72.7 us
    pallas_call x1, Pallas kernels: 79.1 us -> 71.5 us  [local(): pl.pallas_call(kernel, out_shape=(pltpu.VMEM(queries.shape, BF16), pltpu....]
    pallas_call x1, Pallas kernels: 2.23 us -> 1.14 us  [local(): pl.pallas_call(copy_out, out_shape=tuple((sd(r.shape, r.dtype) for r in r...]
where the time goes in v4:
time: 74 us; the launch traced here: 73.3 us
  Pallas kernels  72.7 us (98%)
    pallas_call x1, Pallas kernels, local(): pl.pallas_call(kernel, out_shape=(pltpu.VMEM(queries.shape, BF16), pltpu....  71.5 us

profile of v4, /device:TPU:33, one launch (start us, length us, event | category | flops | bytes accessed | tf_op | source)
XLA Modules:
  0.0 73.3 jit_solution(6469869576401164589)
XLA Ops:
  0.6 71.5 %attention.1 = (bf16[32,8192]{1,0:T(8,128)(2,1)S(1)}, bf16[32,8192]{1,0:T(8,128)(2,1)S(1)}, bf16[32,1024]{1,0:T(8,128)(2,1)S(1)}, bf16[32,1024]{1,0:T(8,128)(2,1...) custom-call(bf16[32,8192]{1,0:T(8,128)(2,1)} %q_ref.1, bf16[32,8192]{1,0:T(8,128)(2,1)} %g_ref.1, ...), custom_call_target="tpu_custom_call" | custom-call | tf_op jit(solution)/shard_map/attention/pallas_call | solution.py:445
  72.2 1.1 %copy_out.1 = (bf16[32,8192]{1,0:T(8,128)(2,1)}, bf16[32,8192]{1,0:T(8,128)(2,1)}, bf16[32,1024]{1,0:T(8,128)(2,1)}, bf16[32,1024]{1,0:T(8,128)(2,1)}, f32[256,128]{1,0:T(8,128)}, /*index=5*/f32[256,128]{1,0:T(8,128)}) custom-call(bf16[32,8192]{1,0:T(8,128)(2,1)S(1)} %get-tuple-element.12.refs_0_, bf16[32,8192]{1,0:T(8,128)(2,1)S(1)} %get-tuple-element.13.refs_1_, ...), custom_call_target="tpu_custom_call" | custom-call | tf_op jit(solution)/shard_map/copy_out/pallas_call | solution.py:489

commit v5 on v4

--- a/solution.py
+++ b/solution.py
@@ -25,7 +25,8 @@
 CUTS = (2, 3, 4, 4)
 LAG = 1
 VMEM_MIB = 56
-ORDER_OUT = (4, 3, 5, 2, 6, 1, 7)
+FIRST = 1
+ORDER_OUT = (1, 2, 3, 4, 5, 6, 7)
 MESH = pl.DeviceIdType.MESH
 SCALE = 1.0 / math.sqrt(HD)
 LOG2E = math.log2(math.e)
@@ -42,10 +43,10 @@
 
 
 def kernel(
-    q_ref, g_ref, k_ref, v_ref, dk_ref, dv_ref, cite_v_ref, cite_ref, list_ref,
+    q_ref, g_ref, k_ref, v_ref, dk_ref, dv_ref, cite_hbm, list_hbm,
     att_ref, qg_ref, kg_ref, vg_ref, dkg_ref, dvg_ref,
     qw, gw, kw, vw, ag, sel, pool, cat, cat_t, acc, att, dq, kv_out, gs, gr, s1, r1, zs, zr,
-    par_v, par_ref, pos_ref, par_sem, own_q, own_doc, kv_s, kv_r, head_s, head_r, z_s, z_r, one_s, one_r, two_s, two_r,
+    open_sem, cite_v_ref, cite_ref, list_ref, small_sem, par_v, par_ref, pos_ref, par_sem, own_q, own_doc, kv_s, kv_r, head_s, head_r, z_s, z_r, one_s, one_r, two_s, two_r,
     kvo_s, kvo_r, out_s, out_r, out_l, two_bs, two_br, one_bs, one_br, zb_s, zb_r,
 ):
     roll = lax.axis_index("roll")
@@ -79,19 +80,34 @@
         pltpu.make_async_copy(ref, ref, sem).wait()
 
     barrier = pltpu.get_barrier_semaphore()
-    partners = [z_dev]
-    partners += [first(t, d) for t in range(2) for d in range(1, size[t])]
+    partners = [first(t, d) for t in range(2) for d in range(1, size[t])]
     partners += [(roll, lax.rem(head + k, NH)) for k in range(1, NH)]
     for dev in partners:
         pl.semaphore_signal(barrier, inc=1, device_id=dev, device_id_type=MESH)
-
-    pl.semaphore_wait(barrier, len(partners))
-
-    z_copy = []
-    for t in range(2):
-        c = remote(docs[t], ag.at[t, 1, place[t]], z_s.at[t], z_r.at[t], z_dev)
+    small = [
+        pltpu.make_async_copy(cite_hbm, cite_v_ref, small_sem.at[0]),
+        pltpu.make_async_copy(cite_hbm, cite_ref, small_sem.at[1]),
+        pltpu.make_async_copy(list_hbm, list_ref, small_sem.at[2]),
+    ]
+    for c in small:
         c.start()
-        z_copy.append(c)
+    gate, other_gate = (NH - 1) * (1 - zh), (NH - 1) * zh
+    pl.semaphore_signal(
+        barrier, inc=1, device_id=(roll_of(x, y, 1 - zh), other_gate), device_id_type=MESH
+    )
+
+    @pl.when(head == gate)
+    def _():
+        pl.semaphore_wait(barrier, len(partners) + NH)
+        for k in range(1, NH):
+            pl.semaphore_signal(
+                open_sem, inc=1, device_id=(roll, lax.rem(head + k, NH)), device_id_type=MESH
+            )
+
+    @pl.when(head != gate)
+    def _():
+        pl.semaphore_wait(barrier, len(partners))
+
     for t in range(2):
         for d in range(1, size[t]):
             c = remote(
@@ -140,8 +156,21 @@
                 chunk_copy(k, i, j).start()
         return 0
 
-    lax.fori_loop(0, STEPS, send_chunks, 0)
-
+    lax.fori_loop(0, FIRST, send_chunks, 0)
+
+    @pl.when(head != gate)
+    def _():
+        pl.semaphore_wait(open_sem, 1)
+
+    z_copy = []
+    for t in range(2):
+        c = remote(docs[t], ag.at[t, 1, place[t]], z_s.at[t], z_r.at[t], z_dev)
+        c.start()
+        z_copy.append(c)
+    lax.fori_loop(FIRST, STEPS, send_chunks, 0)
+
+    for c in small:
+        c.wait()
     cites = cite_v_ref[...]
     rolls = 2 * NX * NY
     owner_at = lax.broadcasted_iota(jnp.int32, (rolls, rolls), 0)
@@ -295,11 +324,8 @@
         for i, ref in enumerate((qw, gw)):
             landed(ref.at[0:others, pl.ds(pl.multiple_of(j * PAIR, PAIR), PAIR)], head_r.at[i, j])
 
-        def per_block(b, _):
-            compute(b, j)
-            return 0
-
-        lax.fori_loop(0, 2, per_block, 0)
+        compute(0, j)
+        compute(1, j)
         @pl.when((j >= LAG) & (j < CUTS[0] + LAG))
         def _():
             send_back(j - LAG, 0)
@@ -319,7 +345,7 @@
         for a in range(size[t]):
             step(a, 0)
 
-    for p in (1, 0):
+    def send_two(p):
         for d in range(1, NX):
             for t in range(2):
                 b = lax.rem(place[1 - t] + d, size[1 - t])
@@ -329,12 +355,18 @@
                     two_bs.at[t, p], two_br.at[t, p], second(t, d),
                 )
                 c.start()
-    lax.fori_loop(CUTS[0], CUTS[1], send_back, 0)
-    for p in (1, 0):
+
+    def own_two(p):
         for t in range(2):
             b = place[1 - t]
             prepare(t, p, b)
             gr[t, p, b] = gs[t, p, b]
+
+    send_two(1)
+    send_two(0)
+    lax.fori_loop(CUTS[0], CUTS[1], send_back, 0)
+    own_two(1)
+    own_two(0)
 
     for t in range(2):
         total = (acc[t, 0, LIST:NONE] + acc[t, 1, LIST:NONE]).reshape(QTOK, HD)
@@ -438,7 +470,6 @@
     n = max(NX, NY)
     any_spec = pl.BlockSpec(memory_space=pltpu.HBM)
     vmem = pl.BlockSpec(memory_space=pltpu.VMEM)
-    smem = pl.BlockSpec(memory_space=pltpu.SMEM)
     dma = pltpu.SemaphoreType.DMA
     blk = (BLOCK, HD)
     sd = jax.ShapeDtypeStruct
@@ -449,7 +480,7 @@
             pltpu.VMEM(keys.shape, BF16), pltpu.VMEM(keys.shape, BF16),
             pltpu.VMEM(doc_keys.shape, F32), pltpu.VMEM(doc_keys.shape, F32),
         ),
-        in_specs=[any_spec] * 6 + [vmem, smem, smem],
+        in_specs=[any_spec] * 8,
         out_specs=(vmem,) * 6,
         scratch_shapes=[
             pltpu.VMEM((QTOK, WIDE), BF16),
@@ -471,6 +502,11 @@
             pltpu.VMEM((2, 2, n, 2 * BLOCK, HD), BF16),
             pltpu.VMEM((2, 2 * BLOCK, HD), BF16),
             pltpu.VMEM((2, 2 * BLOCK, HD), BF16),
+            pltpu.SemaphoreType.REGULAR,
+            pltpu.VMEM(citations.shape[::-1], jnp.int32),
+            pltpu.SMEM(citations.shape[::-1], jnp.int32),
+            pltpu.SMEM(block_lists.shape, jnp.int32),
+            dma((3,)),
             pltpu.VMEM((2 * NX * NY, HD), F32),
             pltpu.SMEM((2 * NX * NY, HD), F32),
             pltpu.SMEM((2, 2 * NX * NY), jnp.int32),
@@ -485,7 +521,7 @@
             collective_id=0, has_side_effects=True, vmem_limit_bytes=VMEM_MIB * 2**20
         ),
         name="attention",
-    )(*[pltpu.with_memory_space_constraint(r, pltpu.HBM) for r in (queries, cotangent, keys, values, doc_keys, doc_values)], citations.T, citations.T, block_lists)
+    )(*[pltpu.with_memory_space_constraint(r, pltpu.HBM) for r in (queries, cotangent, keys, values, doc_keys, doc_values, citations.T, block_lists)])
     return pl.pallas_call(
         copy_out,
         out_shape=tuple(sd(r.shape, r.dtype) for r in results),

time: 74 us -> 71.6 us (0.968)
  Pallas kernels: 72.7 us -> 70.3 us
    pallas_call x1, Pallas kernels: 71.5 us -> 69.1 us  [local(): pl.pallas_call(kernel, out_shape=(pltpu.VMEM(queries.shape, BF16), pltpu....]
where the time goes in v5:
time: 71.6 us; the launch traced here: 70.9 us
  Pallas kernels  70.3 us (98%)
    pallas_call x1, Pallas kernels, local(): pl.pallas_call(kernel, out_shape=(pltpu.VMEM(queries.shape, BF16), pltpu....  69.1 us

profile of v5, /device:TPU:33, one launch (start us, length us, event | category | flops | bytes accessed | tf_op | source)
XLA Modules:
  0.0 70.9 jit_solution(15781139020380254176)
XLA Ops:
  0.6 69.1 %attention.1 = (bf16[32,8192]{1,0:T(8,128)(2,1)S(1)}, bf16[32,8192]{1,0:T(8,128)(2,1)S(1)}, bf16[32,1024]{1,0:T(8,128)(2,1)S(1)}, bf16[32,1024]{1,0:T(8,128)(2,1...) custom-call(bf16[32,8192]{1,0:T(8,128)(2,1)} %q_ref.1, bf16[32,8192]{1,0:T(8,128)(2,1)} %g_ref.1, ...), custom_call_target="tpu_custom_call" | custom-call | tf_op jit(solution)/shard_map/attention/pallas_call | solution.py:476
  69.8 1.1 %copy_out.1 = (bf16[32,8192]{1,0:T(8,128)(2,1)}, bf16[32,8192]{1,0:T(8,128)(2,1)}, bf16[32,1024]{1,0:T(8,128)(2,1)}, bf16[32,1024]{1,0:T(8,128)(2,1)}, f32[256,128]{1,0:T(8,128)}, /*index=5*/f32[256,128]{1,0:T(8,128)}) custom-call(bf16[32,8192]{1,0:T(8,128)(2,1)S(1)} %get-tuple-element.12.refs_0_, bf16[32,8192]{1,0:T(8,128)(2,1)S(1)} %get-tuple-element.13.refs_1_, ...), custom_call_target="tpu_custom_call" | custom-call | tf_op jit(solution)/shard_map/copy_out/pallas_call | solution.py:525

commit v6 on v5

--- a/solution.py
+++ b/solution.py
@@ -26,6 +26,7 @@
 LAG = 1
 VMEM_MIB = 56
 FIRST = 1
+TOGETHER = 3
 ORDER_OUT = (1, 2, 3, 4, 5, 6, 7)
 MESH = pl.DeviceIdType.MESH
 SCALE = 1.0 / math.sqrt(HD)
@@ -119,6 +120,7 @@
         c = pltpu.make_async_copy(docs[t], ag.at[t, 0, place[t]], own_doc.at[t])
         c.start()
         own_docs.append(c)
+    half = head // (NH // 2)
     heads = []
     mine = pl.ds(pl.multiple_of(head * ROWS, ROWS), ROWS)
     moved = ((k_ref, kw, HD), (v_ref, vw, HD), (q_ref, qw, WIDE), (g_ref, gw, WIDE))
@@ -143,7 +145,7 @@
         return remote(
             src.at[:, pl.ds(pl.multiple_of(h * width + j * PAIR, PAIR), PAIR)],
             dst.at[mine, pl.ds(pl.multiple_of(j * PAIR, PAIR), PAIR)],
-            head_s.at[i], head_r.at[i, j], (roll, h),
+            head_s.at[i], head_r.at[i, j, half], (roll, h),
         )
 
     for k in range(1, NH):
@@ -320,19 +322,44 @@
                 chunk_back(k, i, j).start()
         return 0
 
+    def wait_half(j, side):
+        rows = QTOK // 2 if side else QTOK // 2 - ROWS
+        cols = pl.ds(pl.multiple_of(j * PAIR, PAIR), PAIR)
+        for i, ref in enumerate((qw, gw)):
+            landed(ref.at[0:rows, cols], head_r.at[i, j, half if side == 0 else 1 - half])
+
     def per_chunk(j, _):
-        for i, ref in enumerate((qw, gw)):
-            landed(ref.at[0:others, pl.ds(pl.multiple_of(j * PAIR, PAIR), PAIR)], head_r.at[i, j])
-
+        wait_half(j, 0)
+        wait_half(j, 1)
         compute(0, j)
         compute(1, j)
+        after_chunk(j)
+        return 0
+
+    def per_half(j, _):
+        def step(side, _):
+            @pl.when(side == 0)
+            def _():
+                wait_half(j, 0)
+
+            @pl.when(side == 1)
+            def _():
+                wait_half(j, 1)
+
+            compute(half ^ side, j)
+            return 0
+
+        lax.fori_loop(0, 2, step, 0)
+        after_chunk(j)
+        return 0
+
+    def after_chunk(j):
         @pl.when((j >= LAG) & (j < CUTS[0] + LAG))
         def _():
             send_back(j - LAG, 0)
 
-        return 0
-
-    lax.fori_loop(0, STEPS, per_chunk, 0)
+    lax.fori_loop(0, TOGETHER, per_chunk, 0)
+    lax.fori_loop(TOGETHER, STEPS, per_half, 0)
 
     def prepare(t, p, b):
         def step(a, _):
@@ -511,7 +538,7 @@
             pltpu.SMEM((2 * NX * NY, HD), F32),
             pltpu.SMEM((2, 2 * NX * NY), jnp.int32),
             dma((1,)),
-            dma((4,)), dma((2,)), dma((2,)), dma((2,)), dma((2,)), dma((2, STEPS)),
+            dma((4,)), dma((2,)), dma((2,)), dma((2,)), dma((2,)), dma((2, STEPS, 2)),
             dma((2,)), dma((2,)),
             dma((2, 2)), dma((2, 2)), dma((2, 2)), dma((2, 2)),
             dma((2,)), dma((2,)), dma((2,)), dma((2,)), dma((4,)),

time: 71.6 us -> 71.2 us (level)
  no operation moved by 1% of the time
where the time goes in v6:
time: 71.2 us; the launch traced here: 71.1 us
  Pallas kernels  70.4 us (99%)
    pallas_call x1, Pallas kernels, local(): pl.pallas_call(kernel, out_shape=(pltpu.VMEM(queries.shape, BF16), pltpu....  69.3 us

profile of v6, /device:TPU:33, one launch (start us, length us, event | category | flops | bytes accessed | tf_op | source)
XLA Modules:
  0.0 71.1 jit_solution(18125279272447118652)
XLA Ops:
  0.6 69.3 %attention.1 = (bf16[32,8192]{1,0:T(8,128)(2,1)S(1)}, bf16[32,8192]{1,0:T(8,128)(2,1)S(1)}, bf16[32,1024]{1,0:T(8,128)(2,1)S(1)}, bf16[32,1024]{1,0:T(8,128)(2,1...) custom-call(bf16[32,8192]{1,0:T(8,128)(2,1)} %q_ref.1, bf16[32,8192]{1,0:T(8,128)(2,1)} %g_ref.1, ...), custom_call_target="tpu_custom_call" | custom-call | tf_op jit(solution)/shard_map/attention/pallas_call | solution.py:503
  69.9 1.1 %copy_out.1 = (bf16[32,8192]{1,0:T(8,128)(2,1)}, bf16[32,8192]{1,0:T(8,128)(2,1)}, bf16[32,1024]{1,0:T(8,128)(2,1)}, bf16[32,1024]{1,0:T(8,128)(2,1)}, f32[256,128]{1,0:T(8,128)}, /*index=5*/f32[256,128]{1,0:T(8,128)}) custom-call(bf16[32,8192]{1,0:T(8,128)(2,1)S(1)} %get-tuple-element.12.refs_0_, bf16[32,8192]{1,0:T(8,128)(2,1)S(1)} %get-tuple-element.13.refs_1_, ...), custom_call_target="tpu_custom_call" | custom-call | tf_op jit(solution)/shard_map/copy_out/pallas_call | solution.py:552

commit v7 on v6

--- a/solution.py
+++ b/solution.py
@@ -26,7 +26,8 @@
 LAG = 1
 VMEM_MIB = 56
 FIRST = 1
-TOGETHER = 3
+TOGETHER = 2
+ORDER_IN = (4, 3, 5, 2, 6, 1, 7)
 ORDER_OUT = (1, 2, 3, 4, 5, 6, 7)
 MESH = pl.DeviceIdType.MESH
 SCALE = 1.0 / math.sqrt(HD)
@@ -153,7 +154,7 @@
             kv_copy(k, i).start()
 
     def send_chunks(j, _):
-        for k in range(1, NH):
+        for k in ORDER_IN:
             for i in range(2):
                 chunk_copy(k, i, j).start()
         return 0
@@ -337,19 +338,9 @@
         return 0
 
     def per_half(j, _):
-        def step(side, _):
-            @pl.when(side == 0)
-            def _():
-                wait_half(j, 0)
-
-            @pl.when(side == 1)
-            def _():
-                wait_half(j, 1)
-
+        for side in range(2):
+            wait_half(j, side)
             compute(half ^ side, j)
-            return 0
-
-        lax.fori_loop(0, 2, step, 0)
         after_chunk(j)
         return 0
 

time: 71.2 us -> 71.1 us (level)
    pallas_call x1, Pallas kernels: 69.3 us -> 68.5 us  [local(): pl.pallas_call(kernel, out_shape=(pltpu.VMEM(queries.shape, BF16), pltpu....]
where the time goes in v7:
time: 71.1 us; the launch traced here: 70.3 us
  Pallas kernels  69.7 us (98%)
    pallas_call x1, Pallas kernels, local(): pl.pallas_call(kernel, out_shape=(pltpu.VMEM(queries.shape, BF16), pltpu....  68.5 us

profile of v7, /device:TPU:33, one launch (start us, length us, event | category | flops | bytes accessed | tf_op | source)
XLA Modules:
  0.0 70.3 jit_solution(15372010748314762428)
XLA Ops:
  0.6 68.5 %attention.1 = (bf16[32,8192]{1,0:T(8,128)(2,1)S(1)}, bf16[32,8192]{1,0:T(8,128)(2,1)S(1)}, bf16[32,1024]{1,0:T(8,128)(2,1)S(1)}, bf16[32,1024]{1,0:T(8,128)(2,1...) custom-call(bf16[32,8192]{1,0:T(8,128)(2,1)} %q_ref.1, bf16[32,8192]{1,0:T(8,128)(2,1)} %g_ref.1, ...), custom_call_target="tpu_custom_call" | custom-call | tf_op jit(solution)/shard_map/attention/pallas_call | solution.py:494
  69.2 1.1 %copy_out.1 = (bf16[32,8192]{1,0:T(8,128)(2,1)}, bf16[32,8192]{1,0:T(8,128)(2,1)}, bf16[32,1024]{1,0:T(8,128)(2,1)}, bf16[32,1024]{1,0:T(8,128)(2,1)}, f32[256,128]{1,0:T(8,128)}, /*index=5*/f32[256,128]{1,0:T(8,128)}) custom-call(bf16[32,8192]{1,0:T(8,128)(2,1)S(1)} %get-tuple-element.12.refs_0_, bf16[32,8192]{1,0:T(8,128)(2,1)S(1)} %get-tuple-element.13.refs_1_, ...), custom_call_target="tpu_custom_call" | custom-call | tf_op jit(solution)/shard_map/copy_out/pallas_call | solution.py:543
